TPU v7x, 32 devices: a whole 2x2x4 slice. The times are simulated.
32 devices in a mesh: dp: 16 (over z, y, x), expert: 2 (over core).
Axes of the slice: x: 2, y: 2, z: 4, core: 2. Of those that a mesh axis runs over, the one named last changes fastest.
Arguments:
- tokens: bfloat16 [6144, 4096], P('dp'), may hold values from -8 to 8, as said below
- centroids: bfloat16 [512, 4096], P('expert'), may hold values from -8 to 8, as said below
- prices: float32 [512], P('expert'), may hold values from 0 to 259.9922, as said below
- epsilon: float32 [1], replicated, may hold values from 0.125 to 1, as said below
Outputs:
- final_prices: float32 [512], P('expert')
- best_expert: int32 [6144], P('dp')
- holder: int32 [512], P('expert')
- refreshed: bfloat16 [512, 4096], P('expert')
Inputs may be any that keep to these rules, and one draw needn't show every extreme that they name: `tokens`: every entry is a whole number. `centroids`: every entry is a whole number. `prices`: distinct multiples of 1/128. `epsilon`: A multiple of 1/8.
All inputs are finite; a program needn't handle non-finite values.
Results may differ from a plain program's by a relative error of at most 0.001.
Values may be sent and summed in bfloat16 or wider, within the bound.
No kernel may reach another device: no remote copies, remote signals or barrier semaphores. Data moves between devices by JAX's collectives and lax.ppermute only.
A program may use at most 64 MiB of HBM per device.

v0:
```python
import functools

import jax
import jax.numpy as jnp
from jax import lax
from jax.experimental import pallas as pl
from jax.experimental.pallas import tpu as pltpu
from jax.sharding import PartitionSpec as P

ROUNDS = 3

lowest = -1e30
far = 1073741824.0
VMEM = pl.BlockSpec(memory_space=pltpu.VMEM)
SMEM = pl.BlockSpec(memory_space=pltpu.SMEM)
ANY = pl.BlockSpec(memory_space=pl.ANY)


def room(mebibytes):
    return pltpu.CompilerParams(vmem_limit_bytes=mebibytes * 1024 * 1024)


def opening(chunks, place, tokens, centroids, prices, kept, sent, mine, largest, *refs):
    parcels, (tok, cen, acc, sem) = refs[:-4], refs[-4:]
    rows, cols = kept.shape[0], mine.shape[1]
    step = tok.shape[1] // chunks
    copies = []
    for i in range(chunks):
        part = pl.ds(i * step, step)
        copies.append((
            pltpu.make_async_copy(centroids.at[:, part], cen.at[:, part], sem.at[0, i]),
            pltpu.make_async_copy(tokens.at[:, part], tok.at[:, part], sem.at[1, i]),
        ))
    for pair in copies:
        pair[0].start()
        pair[1].start()
    for i, pair in enumerate(copies):
        pair[0].wait()
        pair[1].wait()
        part = slice(i * step, (i + 1) * step)
        product = lax.dot_general(
            tok[:, part], cen[:, part], (((1,), (1,)), ((), ())), preferred_element_type=jnp.float32
        )
        size = jnp.max(jnp.abs(tok[:, part]).reshape(-1, 16, step), axis=0)
        peak = size if i == 0 else jnp.maximum(peak, size)
        if i:
            acc[...] += product
        else:
            acc[...] = product
    peak = jnp.max(peak.astype(jnp.float32), axis=0, keepdims=True)
    largest[...] = jnp.broadcast_to(jnp.max(peak, axis=1, keepdims=True), largest.shape)
    for out, at in ((sent, 1), (kept, 0)):
        row = pl.multiple_of(place[at] * rows, rows)
        out[...] = acc[pl.ds(row, rows), :] * 0.015625 - prices[...]
    mine[...] = cen[:, pl.ds(pl.multiple_of(place[2] * cols, cols), cols)]
    for k, parcel in enumerate(parcels):
        parcel[...] = tok[:, pl.ds(pl.multiple_of(place[3 + k] * cols, cols), cols)]


def choose(values, eps):
    ids = lax.broadcasted_iota(jnp.int32, values.shape, 1).astype(jnp.float32)
    top = jnp.max(values, axis=1, keepdims=True)
    choice = jnp.min(jnp.where(values == top, ids, far), axis=1, keepdims=True)
    claims = ids == choice
    second = jnp.max(jnp.where(claims, lowest, values), axis=1, keepdims=True)
    bids = jnp.where(claims, top - second + eps, -1.0)
    return choice, claims, bids, jnp.max(bids, axis=0, keepdims=True)


def first_round(place, kept, theirs, epsilon, values, out):
    if theirs is None:
        values[...] = kept[...]
    else:
        own = kept.shape[1]
        swapped = place[0] != 0
        values[:, :own] = jnp.where(swapped, theirs[...], kept[...])
        values[:, own:] = jnp.where(swapped, kept[...], theirs[...])
    raised = choose(values[...], epsilon[0])[-1]
    out[...] = jnp.broadcast_to(raised[None], out.shape)


def first_round_whole(place, kept, epsilon, values, out):
    first_round(place, kept, None, epsilon, values, out)


def next_round(values, before, epsilon, bids, out, after):
    total = before[...] + jnp.maximum(jnp.max(bids[...], axis=0), 0.0)
    after[...] = total
    raised = choose(values[...] - total, epsilon[0])[-1]
    out[...] = jnp.broadcast_to(raised[None], out.shape)


def last_round(values, before, epsilon, bids, base, largest, out, after):
    rows, experts = values.shape
    total = before[...] + jnp.maximum(jnp.max(bids[...], axis=0), 0.0)
    after[...] = total
    choice, claims, spread, raised = choose(values[...] - total, epsilon[0])
    token = (base[0] + lax.broadcasted_iota(jnp.int32, (rows, experts), 0)).astype(jnp.float32)
    first = jnp.min(jnp.where(claims & (spread == raised), token, far), axis=0, keepdims=True)
    count = jnp.sum(claims.astype(jnp.float32), axis=0, keepdims=True)
    wide = out.shape[2] - 3 * experts
    lane = lax.broadcasted_iota(jnp.int32, (rows, wide), 1)
    row = lax.broadcasted_iota(jnp.int32, (rows, wide), 0)
    turned = jnp.sum(jnp.where(lane == row, choice, 0.0), axis=0, keepdims=True)
    turned = jnp.where(lane[:1] == rows, largest[:, :1], turned)
    line = jnp.concatenate([raised, first, count, turned], axis=1)
    out[...] = jnp.broadcast_to(line[None], out.shape)


def pass_on(line, *refs):
    pass


def released(line, parcels):
    return pl.pallas_call(
        pass_on,
        out_shape=[jax.ShapeDtypeStruct(p.shape, p.dtype) for p in parcels],
        in_specs=[ANY] * (1 + len(parcels)),
        out_specs=[ANY] * len(parcels),
        input_output_aliases={1 + i: i for i in range(len(parcels))},
        compiler_params=room(4),
        cost_estimate=pl.CostEstimate(flops=1000000000, bytes_accessed=4096, transcendentals=0),
        name="released",
    )(line, *parcels)


def fill(line, value, out):
    out[...] = value[...]


def filled(line, value):
    return pl.pallas_call(
        fill,
        out_shape=jax.ShapeDtypeStruct(value.shape, value.dtype),
        in_specs=[ANY, VMEM],
        out_specs=VMEM,
        compiler_params=room(4),
        cost_estimate=pl.CostEstimate(flops=4000000000, bytes_accessed=4096, transcendentals=0),
        name="filled",
    )(line, value)


def add_up(ne, rows, top, place, info, columns, total_out, short_out):
    height = total_out.shape[0]
    at = info.shape[2] // 128 * 128 - (rows // 128 + 1) * 128
    ids = place[0] + top + lax.broadcasted_iota(jnp.int32, (height, rows), 0)
    ids = ids.astype(jnp.float32)
    total = jnp.zeros(total_out.shape, jnp.float32)
    for k, features in enumerate(columns):
        for c in range(ne):
            chosen = info[place[2 + k] * ne + c, :, at : at + rows]
            hot = jnp.where(ids == chosen, 1.0, 0.0).astype(jnp.bfloat16)
            total += jnp.dot(
                hot, features[c * rows : (c + 1) * rows, :], preferred_element_type=jnp.float32
            )
    total_out[...] = total
    short_out[...] = total.astype(short_out.dtype)


def more_sums(ne, rows, top, place, info, *refs):
    add_up(ne, rows, top, place, info, refs[:-2], *refs[-2:])


def finish(ne, rows, outer, place, info, before, prices, *refs):
    columns, (final, holder, best, counts_out, fits, *sums) = refs[:-7], refs[-7:]
    experts = before.shape[1]
    own = prices.shape[1]
    start = place[0]
    if own % 128 == 0:
        start = pl.multiple_of(start, 128)
        raised = info[:, :, pl.ds(start, own)]
        firsts = info[:, :, pl.ds(pl.multiple_of(experts + start, 128), own)]
        earlier = before[:, pl.ds(start, own)]
        top_bid = jnp.max(raised, axis=0)
        first = jnp.min(jnp.where(raised == top_bid[None], firsts, far), axis=0)
        final[...] = prices[...] + earlier + jnp.maximum(top_bid, 0.0)
        holder[...] = jnp.where(top_bid > 0, first, -1.0).astype(jnp.int32)
    else:
        raised = info[:, :, :experts]
        top_bid = jnp.max(raised, axis=0)
        firsts = jnp.where(raised == top_bid[None], info[:, :, experts : 2 * experts], far)
        final[...] = before[...] + jnp.maximum(top_bid, 0.0)
        holder[...] = jnp.where(top_bid > 0, jnp.min(firsts, axis=0), -1.0).astype(jnp.int32)
    at = 3 * experts
    for c in range(ne):
        mark = info[place[1] * ne + c, :, at : at + rows]
        best[:, c * rows : (c + 1) * rows] = mark.astype(jnp.int32)
    add_up(ne, rows, 0, place, info, columns, *sums)
    share = info.shape[0] // outer
    each = [
        jnp.sum(info[i * share : (i + 1) * share, :, 2 * experts : at], axis=0) for i in range(outer)
    ]
    largest = jnp.max(info[:, :, at + rows : at + rows + 1])
    fullest = jnp.max(functools.reduce(jnp.maximum, each))
    fits[0] = jnp.where(fullest * largest <= 256.0, 1, 0)
    counts = functools.reduce(jnp.add, each)
    expert_row = place[0] + lax.broadcasted_iota(jnp.int32, (own, experts), 0)
    lane = lax.broadcasted_iota(jnp.int32, (own, experts), 1)
    counts = jnp.sum(jnp.where(expert_row == lane, counts, 0.0), axis=1, keepdims=True)
    counts_out[...] = jnp.broadcast_to(jnp.maximum(counts, 1.0), counts_out.shape)


def blend(row, centroids, counts, *refs):
    sums, out = refs[:-1], refs[-1]
    rows, cols = out.shape
    total = functools.reduce(jnp.add, [s[...].astype(jnp.float32) for s in sums])
    old = centroids[row : row + rows, :].astype(jnp.float32)
    share = counts[row : row + rows, :1]
    out[...] = (0.5 * old + 0.5 * total / share).astype(out.dtype)


def assemble(plan, base, *refs):
    pieces, out, sem = refs[: len(plan)], refs[-2], refs[-1]
    cols = pieces[0].shape[-1]
    copies = []
    for piece, (row, slots) in zip(pieces, plan):
        for i, slot in enumerate(slots):
            col = pl.multiple_of(base[slot] * cols, cols)
            copies.append(
                pltpu.make_async_copy(
                    piece.at[i], out.at[pl.ds(row, piece.shape[1]), pl.ds(col, cols)], sem.at[len(copies)]
                )
            )
    for copy in copies:
        copy.start()
    for copy in copies:
        copy.wait()


PARTS = 2
TURNS = ((0, 1), (2, 1))


def spread_out(dp, inner, wide, sums, short, mine, counts):
    bits = inner.bit_length() - 1
    member = lax.axis_index("dp") % inner
    core = lax.axis_index("expert")

    def move(value, masks):
        pairs = [(i * 2 + c, (i ^ masks[c]) * 2 + c) for i in range(dp) for c in range(2)]
        return lax.ppermute(value, ("dp", "expert"), pairs)

    parts = len(sums)
    cols = sums[0].shape[1]
    heights = [s.shape[0] for s in sums]
    tops = [sum(heights[:p]) for p in range(parts)]
    sent = sums if wide else short
    other = [move(s, (inner, inner)) for s in sent] if inner < dp else None
    held = []
    for p in range(parts):
        terms = [sums[p], other[p]] if other else [sums[p]]
        fresh = pl.pallas_call(
            functools.partial(blend, tops[p]),
            out_shape=jax.ShapeDtypeStruct((heights[p], cols), mine.dtype),
            in_specs=[VMEM] * (2 + len(terms)),
            out_specs=VMEM,
            compiler_params=room(4),
            name="blend",
        )(mine, counts, *terms)
        held.append([(fresh[None], [(0, 0)])])

    def join(values):
        return values[0] if len(values) == 1 else jnp.concatenate(values)

    late = [[] for _ in range(parts)]
    for stage in range(bits):
        for p in range(parts):
            masks = [1 << (stage + t) % bits for t in TURNS[p]]

            def onward(entries):
                where = [m for _, ms in entries for m in ms]
                value = move(join([v for v, _ in entries]), masks)
                return value, [(a ^ masks[0], b ^ masks[1]) for a, b in where]

            if stage < bits - 1 or stage < 2:
                held[p].append(onward(held[p]))
            else:
                late[p] = [onward(held[p][:-1]), onward(held[p][-1:])]
    def write(whole, groups):
        pieces, plan, slots = [], [], []
        for p, group in enumerate(groups):
            for value, where in group:
                pieces.append(value)
                plan.append((tops[p], [len(slots) + i for i in range(len(where))]))
                slots += where
        base = jnp.stack([member ^ jnp.where(core == 0, a, b) for a, b in slots]).astype(jnp.int32)
        before = [] if whole is None else [whole]
        return pl.pallas_call(
            functools.partial(assemble, plan),
            out_shape=jax.ShapeDtypeStruct((sum(heights), inner * cols), mine.dtype),
            in_specs=[SMEM] + [VMEM] * len(pieces) + [ANY] * len(before),
            out_specs=ANY,
            scratch_shapes=[pltpu.SemaphoreType.DMA((len(slots),))],
            input_output_aliases={1 + len(pieces): 0} if before else {},
            compiler_params=room(16),
            name="assemble",
        )(base, *pieces, *before)

    whole = write(None, held)
    for p in range(parts):
        if late[p]:
            whole = write(whole, [late[p] if q == p else [] for q in range(parts)])
    return whole


def body(dp, ne, tokens, centroids, prices, epsilon):
    f32 = jnp.float32
    local_tokens, width = tokens.shape
    own = centroids.shape[0]
    experts = own * ne
    devices = dp * ne
    rows = local_tokens // ne
    cols = width // dp
    dp_at, expert_at = lax.axis_index("dp"), lax.axis_index("expert")
    everywhere = ("dp", "expert")
    outer = 2 if ne == 2 and dp % 16 == 0 and dp & (dp - 1) == 0 else 1
    inner = dp // outer
    cols = width // inner
    paired = outer == 2 and cols % 128 == 0 and own % 32 == 0
    swap = [(0, 1), (1, 0)]

    def shape(*sizes, dtype=f32):
        return jax.ShapeDtypeStruct(sizes, dtype)

    line, spread = shape(1, experts), shape(devices, 1, experts)
    at = jnp.stack([expert_at]).astype(jnp.int32)
    if paired:
        half = inner // 2
        chunks = 4
        masks = [(k, inner - 1 - k) for k in range(half)]
        theirs = [dp_at ^ jnp.where(expert_at == 0, *mask) for mask in masks]
        place = [expert_at, 1 - expert_at, dp_at % inner] + [t % inner for t in theirs]
        place = jnp.stack(place).astype(jnp.int32)
        kept, sent, mine, largest, *parcels = pl.pallas_call(
            functools.partial(opening, chunks),
            out_shape=[shape(rows, own)] * 2
            + [shape(own, cols, dtype=centroids.dtype), shape(1, 128)]
            + [shape(local_tokens, cols, dtype=tokens.dtype)] * half,
            in_specs=[SMEM, ANY, ANY, VMEM],
            out_specs=[VMEM] * (4 + half),
            scratch_shapes=[
                pltpu.VMEM(tokens.shape, tokens.dtype),
                pltpu.VMEM(centroids.shape, centroids.dtype),
                pltpu.VMEM((local_tokens, own), f32),
                pltpu.SemaphoreType.DMA((2, chunks)),
            ],
            compiler_params=room(52),
            name="opening",
        )(place, tokens, centroids, prices.reshape(1, own))
        received = lax.ppermute(sent, "expert", swap)
        values, bids = pl.pallas_call(
            first_round,
            out_shape=(shape(rows, experts), spread),
            in_specs=[SMEM, VMEM, VMEM, SMEM],
            out_specs=(VMEM, VMEM),
            compiler_params=room(4),
            name="first_round",
        )(at, kept, received, epsilon)
        columns = [None] * half

        def sent_on(k):
            pairs = [(i * 2 + c, (i ^ masks[k][c]) * 2 + c) for i in range(dp) for c in range(2)]
            columns[k] = lax.ppermute(parcels[k], everywhere, pairs)

        sources = theirs + [dp_at ^ jnp.where(expert_at == 0, *mask[::-1]) for mask in masks]
    else:
        parcels = tokens.reshape(local_tokens, dp, cols).transpose(1, 0, 2)
        columns = lax.all_to_all(parcels, "dp", 0, 0, tiled=True)
        columns = [columns.reshape(dp * local_tokens, cols)[i * local_tokens :][:local_tokens] for i in range(dp)]
        sources = list(range(dp))
        mine = lax.dynamic_slice_in_dim(centroids, dp_at * cols, cols, 1)
        largest = jnp.full((1, 128), jnp.max(jnp.abs(tokens)).astype(f32))
        part = lax.dot_general(
            tokens, centroids, (((1,), (1,)), ((), ())), preferred_element_type=f32
        ) * 0.015625 - prices
        part = lax.all_to_all(part, "expert", 0, 1, tiled=True)
        values, bids = pl.pallas_call(
            first_round_whole,
            out_shape=(shape(rows, experts), spread),
            in_specs=[SMEM, VMEM, SMEM],
            out_specs=(VMEM, VMEM),
            compiler_params=room(4),
            name="first_round",
        )(at, part, epsilon)

    total = jnp.zeros((1, experts), f32)
    waiting = list(range(half))[::-1] if paired else []
    for _ in range(ROUNDS - 2):
        for k in waiting[:-2]:
            sent_on(k)
        waiting = waiting[-2:]
        bids = lax.all_to_all(bids, everywhere, 0, 0, tiled=True)
        bids, total = pl.pallas_call(
            next_round,
            out_shape=(spread, line),
            in_specs=[VMEM, VMEM, SMEM, VMEM],
            out_specs=(VMEM, VMEM),
            compiler_params=room(4),
            name="next_round",
        )(values, total, epsilon, bids)
    if paired:
        parcels[: len(waiting)] = released(total, parcels[: len(waiting)])
    for k in waiting:
        sent_on(k)
    bids = lax.all_to_all(bids, everywhere, 0, 0, tiled=True)
    wide = (rows // 128 + 1) * 128
    largest = filled(total, largest)
    base = (dp_at * local_tokens + expert_at * rows).astype(jnp.int32).reshape(1)
    info, total = pl.pallas_call(
        last_round,
        out_shape=(shape(devices, 1, 3 * experts + wide), line),
        in_specs=[VMEM, VMEM, SMEM, VMEM, SMEM, VMEM],
        out_specs=(VMEM, VMEM),
        compiler_params=room(8),
        name="last_round",
    )(values, total, epsilon, bids, base, largest)
    if paired:
        columns += [lax.ppermute(c, "expert", swap) for c in columns]
    info = lax.all_to_all(info, everywhere, 0, 0, tiled=True)

    place = jnp.stack([expert_at * own, dp_at] + sources).astype(jnp.int32)
    direct = own % 128 == 0
    listed = own if direct else experts
    low = own // 32 * 16 if own % 32 == 0 else own
    heights = [low, own - low] if paired else [own]

    def two(height):
        return (shape(height, cols), shape(height, cols, dtype=jnp.bfloat16))

    final, holder, best, counts, fits, *sums = pl.pallas_call(
        functools.partial(finish, ne, rows, outer),
        out_shape=(
            shape(1, listed),
            shape(1, listed, dtype=jnp.int32),
            shape(1, local_tokens, dtype=jnp.int32),
            shape(own, 128),
            shape(1, dtype=jnp.int32),
        )
        + two(heights[0]),
        in_specs=[SMEM] + [VMEM] * (3 + len(columns)),
        out_specs=(VMEM, VMEM, VMEM, VMEM, SMEM, VMEM, VMEM),
        compiler_params=room(16),
        name="finish",
    )(place, info, total, prices.reshape(1, own), *columns)
    if paired:

        def rest(wide, place, info, columns, sums, best, mine, counts):
            more = pl.pallas_call(
                functools.partial(more_sums, ne, rows, heights[0]),
                out_shape=two(heights[1]),
                in_specs=[SMEM] + [VMEM] * (1 + len(columns)),
                out_specs=(VMEM, VMEM),
                compiler_params=room(16),
                name="more_sums",
            )(place, info, *columns)
            pairs = list(zip(sums, more))
            whole = spread_out(dp, inner, wide, pairs[0], pairs[1], mine, counts)
            return best[0], whole

        best, refreshed = lax.switch(
            fits[0],
            [functools.partial(rest, True), functools.partial(rest, False)],
            place, info, columns, sums, best, mine, counts,
        )
    else:
        best = best[0]
        fresh = 0.5 * mine.astype(f32) + 0.5 * sums[0] / counts[:, :1]
        refreshed = lax.all_gather(fresh.astype(centroids.dtype), "dp", axis=1, tiled=True)
    if direct:
        final, holder = final[0], holder[0]
    else:
        final = prices + lax.dynamic_slice_in_dim(final[0], expert_at * own, own, 0)
        holder = lax.dynamic_slice_in_dim(holder[0], expert_at * own, own, 0)
    return final, best, holder, refreshed


def solution(mesh):
    placed = (P("dp", None), P("expert", None), P("expert"), P())
    return jax.shard_map(
        functools.partial(body, mesh.shape["dp"], mesh.shape["expert"]),
        mesh=mesh,
        in_specs=placed,
        out_specs=(P("expert"), P("dp"), P("expert"), P("expert", None)),
        check_vma=False,
    )
```

profile of v0, /device:TPU:0, one launch (start us, length us, event | category | flops | bytes accessed | tf_op | source)
XLA Modules:
  0.0 88.7 jit_solution(7529578312185738395)
XLA Ops:
  0.7 0.1 stack.182.place
  0.8 0.7 copy-done
  1.5 4.2 %opening.1 = (f32[192,256]{1,0:T(8,128)S(1)}, f32[192,256]{1,0:T(8,128)S(1)}, bf16[256,512]{1,0:T(8,128)(2,1)S(1)}, f32[1,128]{1,0:T(1,128)S(1)}, bf16[384,512]{...) custom-call(s32[7]{0:T(128)S(1)} %stack.182.place, ...), custom_call_target="tpu_custom_call" | custom-call | tf_op jit(solution)/shard_map/opening/pallas_call | solution.py:334
  5.7 0.5 collective-permute-start.20
  6.8 0.4 collective-permute-done.20.theirs
  7.3 0.9 %first_round.1 = (f32[192,512]{1,0:T(8,128)S(1)}, f32[32,1,512]{2,1,0:T(1,128)}) custom-call(s32[1]{0:T(128)} %bitcast.42.place, f32[192,256]{1,0:T(8,128)S(1)} %get-tuple-element.121.kept, f32[192,256]{1,0:T(8,128)S(1)} %collective-permute-done.20.theirs, f32[1]{0:T(128)S(6)} %copy.22.epsilon), custom_call_target="tpu_custom_call" | custom-call | tf_op jit(solution)/shard_map/first_round/pallas_call | solution.py:351
  8.2 7.2 %all-to-all-start = ((f32[32,1,512]{2,1,0:T(1,128)}), f32[32,1,512]{2,1,0:T(1,128)S(1)}, u32[]{:S(2)}, u32[]{:S(2)}) async-start(f32[32,1,512]{2,1,0:T(1,128)} %get-tuple-element.124), calls=%async_computation | async-start | bytes 131072 | tf_op jit(solution)/shard_map/all_to_all | solution.py:392
  15.4 1.8 %collective-permute-start.23 = (bf16[384,512]{1,0:T(8,128)(2,1)S(1)}, bf16[384,512]{1,0:T(8,128)(2,1)S(1)}, u32[]{:S(2)}, u32[]{:S(2)}) collective-permute-start(bf16[384,512]{1,0:T(8,128)(2,1)S(1)} %get-tuple-element.134), channel_id=1, source_target_pairs={{0,4},{1,11},{2,6},{3,9},{4,0},{5,15},{6,2},{7,13},{8,12},{9,3},{1... | collective-permute-start | bytes 1179656 | tf_op jit(solution)/shard_map/ppermute | solution.py:363
  17.3 1.5 %collective-permute-start.24 = (bf16[384,512]{1,0:T(8,128)(2,1)S(1)}, bf16[384,512]{1,0:T(8,128)(2,1)S(1)}, u32[]{:S(2)}, u32[]{:S(2)}) collective-permute-start(bf16[384,512]{1,0:T(8,128)(2,1)S(1)} %get-tuple-element.135), channel_id=1, source_target_pairs={{0,6},{1,9},{2,4},{3,11},{4,2},{5,13},{6,0},{7,15},{8,14},{9,1},{1... | collective-permute-start | bytes 1179656 | tf_op jit(solution)/shard_map/ppermute | solution.py:363
  18.7 4.4 %all-to-all-done.bids = f32[32,1,512]{2,1,0:T(1,128)S(1)} async-done(((f32[32,1,512]{2,1,0:T(1,128)}), f32[32,1,512]{2,1,0:T(1,128)S(1)}, u32[]{:S(2)}, u32[]{:S(2)}) %all-to-all-start) | async-done | bytes 65568 | tf_op jit(solution)/shard_map/all_to_all | solution.py:392
  23.1 0.9 %next_round.1 = (f32[32,1,512]{2,1,0:T(1,128)}, f32[1,512]{1,0:T(1,128)S(1)}) custom-call(f32[192,512]{1,0:T(8,128)S(1)} %get-tuple-element.123.values, f32[1,512]{1,0:T(1,128)S(1)} %broadcast_in_dim.15.before, f32[1]{0:T(128)S(6)} %copy.22.epsilon, f32[32,1,512]{2,1,0:T(1,128)S(1)} %all-to-all-done.bids), custom_call_target="tpu_custom_call" | custom-call | tf_op jit(solution)/shard_map/next_round/pallas_call | solution.py:393
  24.0 2.6 %all-to-all-start.1 = ((f32[32,1,512]{2,1,0:T(1,128)}), f32[32,1,512]{2,1,0:T(1,128)S(1)}, u32[]{:S(2)}, u32[]{:S(2)}) async-start(f32[32,1,512]{2,1,0:T(1,128)} %get-tuple-element.126), calls=%async_computation.1 | async-start | bytes 131072 | tf_op jit(solution)/shard_map/all_to_all | solution.py:405
  26.6 1.4 %collective-permute-start.21 = (bf16[384,512]{1,0:T(8,128)(2,1)S(1)}, bf16[384,512]{1,0:T(8,128)(2,1)}, u32[]{:S(2)}, u32[]{:S(2)}) collective-permute-start(bf16[384,512]{1,0:T(8,128)(2,1)S(1)} %get-tuple-element.132), channel_id=1, source_target_pairs={{0,0},{1,15},{2,2},{3,13},{4,4},{5,11},{6,6},{7,9},{8,8},{9,7},{10... | collective-permute-start | bytes 1179656 | tf_op jit(solution)/shard_map/ppermute | solution.py:363
  28.0 1.6 %collective-permute-start.22 = (bf16[384,512]{1,0:T(8,128)(2,1)S(1)}, bf16[384,512]{1,0:T(8,128)(2,1)}, u32[]{:S(2)}, u32[]{:S(2)}) collective-permute-start(bf16[384,512]{1,0:T(8,128)(2,1)S(1)} %get-tuple-element.133), channel_id=1, source_target_pairs={{0,2},{1,13},{2,0},{3,15},{4,6},{5,9},{6,4},{7,11},{8,10},{9,5},{1... | collective-permute-start | bytes 1179656 | tf_op jit(solution)/shard_map/ppermute | solution.py:363
  29.7 4.4 %all-to-all-done.1.bids = f32[32,1,512]{2,1,0:T(1,128)S(1)} async-done(((f32[32,1,512]{2,1,0:T(1,128)}), f32[32,1,512]{2,1,0:T(1,128)S(1)}, u32[]{:S(2)}, u32[]{:S(2)}) %all-to-all-start.1) | async-done | bytes 65568 | tf_op jit(solution)/shard_map/all_to_all | solution.py:405
  34.0 1.1 %last_round.1 = (f32[32,1,1792]{2,1,0:T(1,128)}, f32[1,512]{1,0:T(1,128)S(1)}) custom-call(f32[192,512]{1,0:T(8,128)S(1)} %get-tuple-element.123.values, f32[1,512]{1,0:T(1,128)S(1)} %get-tuple-element.125.line.before, f32[1]{0:T(128)S(6)} %copy.22.epsilon, f32[32,1,512]{2,1,0:T(1,128)S(1)} %all-to-all-done.1.bids, s32[1]{0:T(128)} %bitcast.50.base, ...), custom_call_target="tpu_custom_call" | custom-call | tf_op jit(solution)/shard_map/last_round/pallas_call | solution.py:409
  35.1 2.6 %all-to-all-start.2 = ((f32[32,1,1792]{2,1,0:T(1,128)}), f32[32,1,1792]{2,1,0:T(1,128)S(1)}, u32[]{:S(2)}, u32[]{:S(2)}) async-start(f32[32,1,1792]{2,1,0:T(1,128)} %get-tuple-element.128), calls=%async_computation.2 | async-start | bytes 458752 | tf_op jit(solution)/shard_map/all_to_all | solution.py:419
  37.7 0.3 collective-permute-start.27
  38.0 0.3 collective-permute-start.28
  38.3 0.2 collective-permute-start.25
  38.5 1.9 %collective-permute-done.22.refs_1_ = bf16[384,512]{1,0:T(8,128)(2,1)} collective-permute-done((bf16[384,512]{1,0:T(8,128)(2,1)S(1)}, bf16[384,512]{1,0:T(8,128)(2,1)}, u32[]{:S(2)}, u32[]{:S(2)}) %collective-permute-start.22) | collective-permute-done | bytes 393248 | tf_op jit(solution)/shard_map/ppermute | solution.py:363
  40.4 2.4 %collective-permute-start.26 = (bf16[384,512]{1,0:T(8,128)(2,1)}, bf16[384,512]{1,0:T(8,128)(2,1)S(1)}, u32[]{:S(2)}, u32[]{:S(2)}) collective-permute-start(bf16[384,512]{1,0:T(8,128)(2,1)} %collective-permute-done.22.refs_1_), channel_id=1, source_target_pairs={{0,1},{1,0},{2,3},{3,2},{4,5},{5,4},{6,7},{7,6},{8,9},{9,8},{10,11... | collective-permute-start | bytes 1179656 | tf_op jit(solution)/shard_map/ppermute | solution.py:418
  42.8 0.1 stack.174.place
  42.9 5.3 %all-to-all-done.2.info = f32[32,1,1792]{2,1,0:T(1,128)S(1)} async-done(((f32[32,1,1792]{2,1,0:T(1,128)}), f32[32,1,1792]{2,1,0:T(1,128)S(1)}, u32[]{:S(2)}, u32[]{:S(2)}) %all-to-all-start.2) | async-done | bytes 229408 | tf_op jit(solution)/shard_map/all_to_all | solution.py:419
  48.2 2.4 %finish.1 = (f32[1,256]{1,0:T(1,128)}, s32[1,256]{1,0:T(1,128)}, s32[1,384]{1,0:T(1,128)S(1)}, f32[256,128]{1,0:T(8,128)S(1)}, s32[1]{0:T(128)}, /*index=5*/f32[128,512]{1,0:T(8,128)S(1)}, bf16[128,512]{1,0:T(8,128)(2,1)S(1)}) custom-call(s32[10]{0:T(128)S(1)} %stack.174.place, f32[32,1,1792]{2,1,0:T(1,128)S(1)} %all-to-all-done.2.info, ...), custom_call_target="tpu_custom_call" | custom-call | tf_op jit(solution)/shard_map/finish/pallas_call | solution.py:430
  51.2 36.9 %conditional.1 = (bf16[256,4096]{1,0:T(8,128)(2,1)}, s32[1,384]{1,0:T(1,128)S(1)}) conditional(s32[]{:T(128)} %bitcast.52, (s32[10]{0:T(128)S(1)}, f32[32,1,1792]{2,1,0:T(1,128)S(1)}, bf16[384,512]{1,0:T(8,128)(2,1)}, bf16[384,512]{1,0:T(8,128)(2,1)}, bf16[384,512]{1,0:T(8,128)(2,1)S(1)}, /*index=5*/bf16[384,512]{1,0:T(8,128)(2,1)S(1)}, ...), branch_computations={%region_0.1_spmd, %region_1.2_spmd} | conditional | flops 262210 | bytes 10486782 | solution.py:460
  51.2 1.0 %collective-permute-start.15 = (bf16[128,512]{1,0:T(8,128)(2,1)S(1)}, bf16[128,512]{1,0:T(8,128)(2,1)S(1)}, u32[]{:S(2)}, u32[]{:S(2)}) collective-permute-start(bf16[128,512]{1,0:T(8,128)(2,1)S(1)} %get-tuple-element.90), channel_id=1, source_target_pairs={{0,16},{1,17},{2,18},{3,19},{4,20},{5,21},{6,22},{7,23},{8,24},{9,... | collective-permute-start | bytes 393224 | tf_op jit(solution)/shard_map/cond/branch_1_fun/ppermute | solution.py:241
  52.3 1.8 %more_sums.3 = (f32[128,512]{1,0:T(8,128)S(1)}, bf16[128,512]{1,0:T(8,128)(2,1)S(1)}) custom-call(s32[10]{0:T(128)S(1)} %get-tuple-element.77.place, f32[32,1,1792]{2,1,0:T(1,128)S(1)} %get-tuple-element.78.info, bf16[384,512]{1,0:T(8,128)(2,1)} %get-tuple-element.79.refs_0_, bf16[384,512]{1,0:T(8,128)(2,1)} %get-tuple-element.80.refs_1_, ...), custom_call_target="tpu_custom_call" | custom-call | tf_op jit(solution)/shard_map/cond/branch_1_fun/more_sums/pallas_call | solution.py:448
  54.1 2.0 %collective-permute-start.10 = (bf16[128,512]{1,0:T(8,128)(2,1)S(1)}, bf16[128,512]{1,0:T(8,128)(2,1)S(1)}, u32[]{:S(2)}, u32[]{:S(2)}) collective-permute-start(bf16[128,512]{1,0:T(8,128)(2,1)S(1)} %get-tuple-element.88), channel_id=1, source_target_pairs={{0,16},{1,17},{2,18},{3,19},{4,20},{5,21},{6,22},{7,23},{8,24},{9,... | collective-permute-start | bytes 393224 | tf_op jit(solution)/shard_map/cond/branch_1_fun/ppermute | solution.py:241
  56.1 6.6 %collective-permute-done.15.refs_1_ = bf16[128,512]{1,0:T(8,128)(2,1)S(1)} collective-permute-done((bf16[128,512]{1,0:T(8,128)(2,1)S(1)}, bf16[128,512]{1,0:T(8,128)(2,1)S(1)}, u32[]{:S(2)}, u32[]{:S(2)}) %collective-permute-start.15) | collective-permute-done | bytes 131104 | tf_op jit(solution)/shard_map/cond/branch_1_fun/ppermute | solution.py:241
  62.8 0.1 blend.7
  62.9 1.5 %collective-permute-start.16 = (bf16[1,128,512]{2,1,0:T(8,128)(2,1)S(1)}, bf16[1,128,512]{2,1,0:T(8,128)(2,1)S(1)}, u32[]{:S(2)}, u32[]{:S(2)}) collective-permute-start(bf16[1,128,512]{2,1,0:T(8,128)(2,1)S(1)} %bitcast.54), channel_id=1, source_target_pairs={{0,2},{1,5},{2,0},{3,7},{4,6},{5,1},{6,4},{7,3},{8,10},{9,13},{10,... | collective-permute-start | bytes 393224 | tf_op jit(solution)/shard_map/cond/branch_1_fun/ppermute | solution.py:241
  64.4 1.0 %collective-permute-done.10.refs_1_ = bf16[128,512]{1,0:T(8,128)(2,1)S(1)} collective-permute-done((bf16[128,512]{1,0:T(8,128)(2,1)S(1)}, bf16[128,512]{1,0:T(8,128)(2,1)S(1)}, u32[]{:S(2)}, u32[]{:S(2)}) %collective-permute-start.10) | collective-permute-done | bytes 131104 | tf_op jit(solution)/shard_map/cond/branch_1_fun/ppermute | solution.py:241
  65.3 0.1 blend.6
  65.5 2.4 %collective-permute-done.16.refs_1_ = bf16[1,128,512]{2,1,0:T(8,128)(2,1)S(1)} collective-permute-done((bf16[1,128,512]{2,1,0:T(8,128)(2,1)S(1)}, bf16[1,128,512]{2,1,0:T(8,128)(2,1)S(1)}, u32[]{:S(2)}, u32[]{:S(2)}) %collective-permute-start.16) | collective-permute-done | bytes 131104 | tf_op jit(solution)/shard_map/cond/branch_1_fun/ppermute | solution.py:241
  68.0 1.7 %collective-permute-start.18 = (bf16[2,128,512]{2,1,0:T(8,128)(2,1)S(1)}, bf16[2,128,512]{2,1,0:T(8,128)(2,1)S(1)}, u32[]{:S(2)}, u32[]{:S(2)}) collective-permute-start(bf16[2,128,512]{2,1,0:T(8,128)(2,1)S(1)} %pad_maximum_fusion.3), channel_id=1, source_target_pairs={{0,4},{1,9},{2,6},{3,11},{4,0},{5,13},{6,2},{7,15},{8,12},{9,1},{1... | collective-permute-start | bytes 786440 | tf_op jit(solution)/shard_map/cond/branch_1_fun/ppermute | solution.py:241
  69.6 1.5 %collective-permute-done.11.refs_4_ = bf16[1,128,512]{2,1,0:T(8,128)(2,1)S(1)} collective-permute-done((bf16[1,128,512]{2,1,0:T(8,128)(2,1)S(1)}, bf16[1,128,512]{2,1,0:T(8,128)(2,1)S(1)}, u32[]{:S(2)}, u32[]{:S(2)}) %collective-permute-start.11) | collective-permute-done | bytes 131104 | tf_op jit(solution)/shard_map/cond/branch_1_fun/ppermute | solution.py:241
  71.1 1.9 %collective-permute-start.13 = (bf16[2,128,512]{2,1,0:T(8,128)(2,1)S(1)}, bf16[2,128,512]{2,1,0:T(8,128)(2,1)S(1)}, u32[]{:S(2)}, u32[]{:S(2)}) collective-permute-start(bf16[2,128,512]{2,1,0:T(8,128)(2,1)S(1)} %pad_maximum_fusion.2), channel_id=1, source_target_pairs={{0,2},{1,9},{2,0},{3,11},{4,6},{5,13},{6,4},{7,15},{8,10},{9,1},{1... | collective-permute-start | bytes 786440 | tf_op jit(solution)/shard_map/cond/branch_1_fun/ppermute | solution.py:241
  73.1 1.3 %collective-permute-done.18.refs_2_ = bf16[2,128,512]{2,1,0:T(8,128)(2,1)S(1)} collective-permute-done((bf16[2,128,512]{2,1,0:T(8,128)(2,1)S(1)}, bf16[2,128,512]{2,1,0:T(8,128)(2,1)S(1)}, u32[]{:S(2)}, u32[]{:S(2)}) %collective-permute-start.18) | collective-permute-done | bytes 262176 | tf_op jit(solution)/shard_map/cond/branch_1_fun/ppermute | solution.py:241
  74.4 0.7 collective-permute-start.19
  75.1 0.9 collective-permute-start.12
  76.0 4.4 %collective-permute-done.13.refs_5_ = bf16[2,128,512]{2,1,0:T(8,128)(2,1)S(1)} collective-permute-done((bf16[2,128,512]{2,1,0:T(8,128)(2,1)S(1)}, bf16[2,128,512]{2,1,0:T(8,128)(2,1)S(1)}, u32[]{:S(2)}, u32[]{:S(2)}) %collective-permute-start.13) | collective-permute-done | bytes 262176 | tf_op jit(solution)/shard_map/cond/branch_1_fun/ppermute | solution.py:241
  80.4 1.7 %collective-permute-start.14 = (bf16[2,128,512]{2,1,0:T(8,128)(2,1)S(1)}, bf16[2,128,512]{2,1,0:T(8,128)(2,1)S(1)}, u32[]{:S(2)}, u32[]{:S(2)}) collective-permute-start(bf16[2,128,512]{2,1,0:T(8,128)(2,1)S(1)} %collective-permute-done.13.refs_5_), channel_id=1, source_target_pairs={{0,4},{1,3},{2,6},{3,1},{4,0},{5,7},{6,2},{7,5},{8,12},{9,11},{10,... | collective-permute-start | bytes 786440 | tf_op jit(solution)/shard_map/cond/branch_1_fun/ppermute | solution.py:241
  82.2 1.6 %assemble.9.refs_2_ = bf16[256,4096]{1,0:T(8,128)(2,1)} custom-call(s32[8]{0:T(128)S(1)} %stack.144.base, bf16[1,128,512]{2,1,0:T(8,128)(2,1)S(1)} %bitcast.56, bf16[1,128,512]{2,1,0:T(8,128)(2,1)S(1)} %collective-permute-done.16.refs_1_, bf16[2,128,512]{2,1,0:T(8,128)(2,1)S(1)} %collective-permute-done.18.refs_2_, bf16[1,128,512]{2,1,0:T(8,128)(2,1)S(1)} %bitcast.59, ...), custom_call_target="tpu_custom_call" | custom-call | tf_op jit(solution)/shard_map/cond/branch_1_fun/assemble/pallas_call | solution.py:288
  83.8 1.4 %assemble.10.refs_2_ = bf16[256,4096]{1,0:T(8,128)(2,1)} custom-call(s32[4]{0:T(128)S(1)} %get-tuple-element.149.base, bf16[2,128,512]{2,1,0:T(8,128)(2,1)S(1)} %collective-permute-done.17.refs_0_, bf16[2,128,512]{2,1,0:T(8,128)(2,1)S(1)} %collective-permute-done.19.refs_1_, bf16[256,4096]{1,0:T(8,128)(2,1)} %assemble.9.refs_2_), custom_call_target="tpu_custom_call", output_to_operand_aliasing={{}: (3, {})} | custom-call | tf_op jit(solution)/shard_map/cond/branch_1_fun/assemble/pallas_call | solution.py:288
  85.2 1.5 %collective-permute-done.14.refs_1_ = bf16[2,128,512]{2,1,0:T(8,128)(2,1)S(1)} collective-permute-done((bf16[2,128,512]{2,1,0:T(8,128)(2,1)S(1)}, bf16[2,128,512]{2,1,0:T(8,128)(2,1)S(1)}, u32[]{:S(2)}, u32[]{:S(2)}) %collective-permute-start.14) | collective-permute-done | bytes 262176 | tf_op jit(solution)/shard_map/cond/branch_1_fun/ppermute | solution.py:241
  86.7 1.4 %assemble.11 = bf16[256,4096]{1,0:T(8,128)(2,1)} custom-call(s32[4]{0:T(128)S(1)} %get-tuple-element.148.base, bf16[2,128,512]{2,1,0:T(8,128)(2,1)S(1)} %collective-permute-done.12.refs_0_, bf16[2,128,512]{2,1,0:T(8,128)(2,1)S(1)} %collective-permute-done.14.refs_1_, bf16[256,4096]{1,0:T(8,128)(2,1)} %assemble.10.refs_2_), custom_call_target="tpu_custom_call", output_to_operand_aliasing={{}: (3, {})} | custom-call | tf_op jit(solution)/shard_map/cond/branch_1_fun/assemble/pallas_call | solution.py:288
  88.1 0.6 reduce
  (22 shorter events, 0.3 us)
Async XLA Ops:
  0.8 0.7 copy-start
  5.7 1.6 %collective-permute-start.20 = (f32[192,256]{1,0:T(8,128)S(1)}, f32[192,256]{1,0:T(8,128)S(1)}, u32[]{:S(2)}, u32[]{:S(2)}) collective-permute-start(f32[192,256]{1,0:T(8,128)S(1)} %get-tuple-element.122), channel_id=1, source_target_pairs={{0,1},{1,0},{2,3},{3,2},{4,5},{5,4},{6,7},{7,6},{8,9},{9,8},{10,11... | collective-permute-start | bytes 589832 | tf_op jit(solution)/shard_map/ppermute | solution.py:350
  8.2 14.9 %all-to-all-start = ((f32[32,1,512]{2,1,0:T(1,128)}), f32[32,1,512]{2,1,0:T(1,128)S(1)}, u32[]{:S(2)}, u32[]{:S(2)}) async-start(f32[32,1,512]{2,1,0:T(1,128)} %get-tuple-element.124), calls=%async_computation | async-start | bytes 131072 | tf_op jit(solution)/shard_map/all_to_all | solution.py:392
  15.4 22.3 %collective-permute-start.23 = (bf16[384,512]{1,0:T(8,128)(2,1)S(1)}, bf16[384,512]{1,0:T(8,128)(2,1)S(1)}, u32[]{:S(2)}, u32[]{:S(2)}) collective-permute-start(bf16[384,512]{1,0:T(8,128)(2,1)S(1)} %get-tuple-element.134), channel_id=1, source_target_pairs={{0,4},{1,11},{2,6},{3,9},{4,0},{5,15},{6,2},{7,13},{8,12},{9,3},{1... | collective-permute-start | bytes 1179656 | tf_op jit(solution)/shard_map/ppermute | solution.py:363
  17.3 20.7 %collective-permute-start.24 = (bf16[384,512]{1,0:T(8,128)(2,1)S(1)}, bf16[384,512]{1,0:T(8,128)(2,1)S(1)}, u32[]{:S(2)}, u32[]{:S(2)}) collective-permute-start(bf16[384,512]{1,0:T(8,128)(2,1)S(1)} %get-tuple-element.135), channel_id=1, source_target_pairs={{0,6},{1,9},{2,4},{3,11},{4,2},{5,13},{6,0},{7,15},{8,14},{9,1},{1... | collective-permute-start | bytes 1179656 | tf_op jit(solution)/shard_map/ppermute | solution.py:363
  24.0 10.0 %all-to-all-start.1 = ((f32[32,1,512]{2,1,0:T(1,128)}), f32[32,1,512]{2,1,0:T(1,128)S(1)}, u32[]{:S(2)}, u32[]{:S(2)}) async-start(f32[32,1,512]{2,1,0:T(1,128)} %get-tuple-element.126), calls=%async_computation.1 | async-start | bytes 131072 | tf_op jit(solution)/shard_map/all_to_all | solution.py:405
  26.6 11.7 %collective-permute-start.21 = (bf16[384,512]{1,0:T(8,128)(2,1)S(1)}, bf16[384,512]{1,0:T(8,128)(2,1)}, u32[]{:S(2)}, u32[]{:S(2)}) collective-permute-start(bf16[384,512]{1,0:T(8,128)(2,1)S(1)} %get-tuple-element.132), channel_id=1, source_target_pairs={{0,0},{1,15},{2,2},{3,13},{4,4},{5,11},{6,6},{7,9},{8,8},{9,7},{10... | collective-permute-start | bytes 1179656 | tf_op jit(solution)/shard_map/ppermute | solution.py:363
  28.0 12.4 %collective-permute-start.22 = (bf16[384,512]{1,0:T(8,128)(2,1)S(1)}, bf16[384,512]{1,0:T(8,128)(2,1)}, u32[]{:S(2)}, u32[]{:S(2)}) collective-permute-start(bf16[384,512]{1,0:T(8,128)(2,1)S(1)} %get-tuple-element.133), channel_id=1, source_target_pairs={{0,2},{1,13},{2,0},{3,15},{4,6},{5,9},{6,4},{7,11},{8,10},{9,5},{1... | collective-permute-start | bytes 1179656 | tf_op jit(solution)/shard_map/ppermute | solution.py:363
  29.7 18.5 %copy-start.1 = (f32[256]{0:T(256)S(1)}, f32[256]{0:T(256)}, u32[]{:S(2)}) copy-start(f32[256]{0:T(256)} %param.8) | copy-start | bytes 3076
  35.1 13.0 %all-to-all-start.2 = ((f32[32,1,1792]{2,1,0:T(1,128)}), f32[32,1,1792]{2,1,0:T(1,128)S(1)}, u32[]{:S(2)}, u32[]{:S(2)}) async-start(f32[32,1,1792]{2,1,0:T(1,128)} %get-tuple-element.128), calls=%async_computation.2 | async-start | bytes 458752 | tf_op jit(solution)/shard_map/all_to_all | solution.py:419
  37.7 5.2 %collective-permute-start.27 = (bf16[384,512]{1,0:T(8,128)(2,1)S(1)}, bf16[384,512]{1,0:T(8,128)(2,1)S(1)}, u32[]{:S(2)}, u32[]{:S(2)}) collective-permute-start(bf16[384,512]{1,0:T(8,128)(2,1)S(1)} %collective-permute-done.23.refs_2_), channel_id=1, source_target_pairs={{0,1},{1,0},{2,3},{3,2},{4,5},{5,4},{6,7},{7,6},{8,9},{9,8},{10,11... | collective-permute-start | bytes 1179656 | tf_op jit(solution)/shard_map/ppermute | solution.py:418
  38.0 4.9 %collective-permute-start.28 = (bf16[384,512]{1,0:T(8,128)(2,1)S(1)}, bf16[384,512]{1,0:T(8,128)(2,1)S(1)}, u32[]{:S(2)}, u32[]{:S(2)}) collective-permute-start(bf16[384,512]{1,0:T(8,128)(2,1)S(1)} %collective-permute-done.24.refs_3_), channel_id=1, source_target_pairs={{0,1},{1,0},{2,3},{3,2},{4,5},{5,4},{6,7},{7,6},{8,9},{9,8},{10,11... | collective-permute-start | bytes 1179656 | tf_op jit(solution)/shard_map/ppermute | solution.py:418
  38.3 9.9 %collective-permute-start.25 = (bf16[384,512]{1,0:T(8,128)(2,1)}, bf16[384,512]{1,0:T(8,128)(2,1)S(1)}, u32[]{:S(2)}, u32[]{:S(2)}) collective-permute-start(bf16[384,512]{1,0:T(8,128)(2,1)} %collective-permute-done.21.refs_0_), channel_id=1, source_target_pairs={{0,1},{1,0},{2,3},{3,2},{4,5},{5,4},{6,7},{7,6},{8,9},{9,8},{10,11... | collective-permute-start | bytes 1179656 | tf_op jit(solution)/shard_map/ppermute | solution.py:418
  40.4 7.8 %collective-permute-start.26 = (bf16[384,512]{1,0:T(8,128)(2,1)}, bf16[384,512]{1,0:T(8,128)(2,1)S(1)}, u32[]{:S(2)}, u32[]{:S(2)}) collective-permute-start(bf16[384,512]{1,0:T(8,128)(2,1)} %collective-permute-done.22.refs_1_), channel_id=1, source_target_pairs={{0,1},{1,0},{2,3},{3,2},{4,5},{5,4},{6,7},{7,6},{8,9},{9,8},{10,11... | collective-permute-start | bytes 1179656 | tf_op jit(solution)/shard_map/ppermute | solution.py:418
  51.2 11.5 %collective-permute-start.15 = (bf16[128,512]{1,0:T(8,128)(2,1)S(1)}, bf16[128,512]{1,0:T(8,128)(2,1)S(1)}, u32[]{:S(2)}, u32[]{:S(2)}) collective-permute-start(bf16[128,512]{1,0:T(8,128)(2,1)S(1)} %get-tuple-element.90), channel_id=1, source_target_pairs={{0,16},{1,17},{2,18},{3,19},{4,20},{5,21},{6,22},{7,23},{8,24},{9,... | collective-permute-start | bytes 393224 | tf_op jit(solution)/shard_map/cond/branch_1_fun/ppermute | solution.py:241
  54.1 11.2 %collective-permute-start.10 = (bf16[128,512]{1,0:T(8,128)(2,1)S(1)}, bf16[128,512]{1,0:T(8,128)(2,1)S(1)}, u32[]{:S(2)}, u32[]{:S(2)}) collective-permute-start(bf16[128,512]{1,0:T(8,128)(2,1)S(1)} %get-tuple-element.88), channel_id=1, source_target_pairs={{0,16},{1,17},{2,18},{3,19},{4,20},{5,21},{6,22},{7,23},{8,24},{9,... | collective-permute-start | bytes 393224 | tf_op jit(solution)/shard_map/cond/branch_1_fun/ppermute | solution.py:241
  62.9 5.0 %collective-permute-start.16 = (bf16[1,128,512]{2,1,0:T(8,128)(2,1)S(1)}, bf16[1,128,512]{2,1,0:T(8,128)(2,1)S(1)}, u32[]{:S(2)}, u32[]{:S(2)}) collective-permute-start(bf16[1,128,512]{2,1,0:T(8,128)(2,1)S(1)} %bitcast.54), channel_id=1, source_target_pairs={{0,2},{1,5},{2,0},{3,7},{4,6},{5,1},{6,4},{7,3},{8,10},{9,13},{10,... | collective-permute-start | bytes 393224 | tf_op jit(solution)/shard_map/cond/branch_1_fun/ppermute | solution.py:241
  65.4 5.7 %collective-permute-start.11 = (bf16[1,128,512]{2,1,0:T(8,128)(2,1)S(1)}, bf16[1,128,512]{2,1,0:T(8,128)(2,1)S(1)}, u32[]{:S(2)}, u32[]{:S(2)}) collective-permute-start(bf16[1,128,512]{2,1,0:T(8,128)(2,1)S(1)} %bitcast.57), channel_id=1, source_target_pairs={{0,8},{1,5},{2,10},{3,7},{4,12},{5,1},{6,14},{7,3},{8,0},{9,13},{1... | collective-permute-start | bytes 393224 | tf_op jit(solution)/shard_map/cond/branch_1_fun/ppermute | solution.py:241
  68.0 6.4 %collective-permute-start.18 = (bf16[2,128,512]{2,1,0:T(8,128)(2,1)S(1)}, bf16[2,128,512]{2,1,0:T(8,128)(2,1)S(1)}, u32[]{:S(2)}, u32[]{:S(2)}) collective-permute-start(bf16[2,128,512]{2,1,0:T(8,128)(2,1)S(1)} %pad_maximum_fusion.3), channel_id=1, source_target_pairs={{0,4},{1,9},{2,6},{3,11},{4,0},{5,13},{6,2},{7,15},{8,12},{9,1},{1... | collective-permute-start | bytes 786440 | tf_op jit(solution)/shard_map/cond/branch_1_fun/ppermute | solution.py:241
  71.1 9.2 %collective-permute-start.13 = (bf16[2,128,512]{2,1,0:T(8,128)(2,1)S(1)}, bf16[2,128,512]{2,1,0:T(8,128)(2,1)S(1)}, u32[]{:S(2)}, u32[]{:S(2)}) collective-permute-start(bf16[2,128,512]{2,1,0:T(8,128)(2,1)S(1)} %pad_maximum_fusion.2), channel_id=1, source_target_pairs={{0,2},{1,9},{2,0},{3,11},{4,6},{5,13},{6,4},{7,15},{8,10},{9,1},{1... | collective-permute-start | bytes 786440 | tf_op jit(solution)/shard_map/cond/branch_1_fun/ppermute | solution.py:241
  73.1 10.7 %collective-permute-start.17 = (bf16[2,128,512]{2,1,0:T(8,128)(2,1)S(1)}, bf16[2,128,512]{2,1,0:T(8,128)(2,1)S(1)}, u32[]{:S(2)}, u32[]{:S(2)}) collective-permute-start(bf16[2,128,512]{2,1,0:T(8,128)(2,1)S(1)} %pad_maximum_fusion.3), channel_id=1, source_target_pairs={{0,8},{1,3},{2,10},{3,1},{4,12},{5,7},{6,14},{7,5},{8,0},{9,11},{1... | collective-permute-start | bytes 786440 | tf_op jit(solution)/shard_map/cond/branch_1_fun/ppermute | solution.py:241
  74.4 9.4 %collective-permute-start.19 = (bf16[2,128,512]{2,1,0:T(8,128)(2,1)S(1)}, bf16[2,128,512]{2,1,0:T(8,128)(2,1)S(1)}, u32[]{:S(2)}, u32[]{:S(2)}) collective-permute-start(bf16[2,128,512]{2,1,0:T(8,128)(2,1)S(1)} %collective-permute-done.18.refs_2_), channel_id=1, source_target_pairs={{0,8},{1,3},{2,10},{3,1},{4,12},{5,7},{6,14},{7,5},{8,0},{9,11},{1... | collective-permute-start | bytes 786440 | tf_op jit(solution)/shard_map/cond/branch_1_fun/ppermute | solution.py:241
  75.1 10.1 %collective-permute-start.12 = (bf16[2,128,512]{2,1,0:T(8,128)(2,1)S(1)}, bf16[2,128,512]{2,1,0:T(8,128)(2,1)S(1)}, u32[]{:S(2)}, u32[]{:S(2)}) collective-permute-start(bf16[2,128,512]{2,1,0:T(8,128)(2,1)S(1)} %pad_maximum_fusion.2), channel_id=1, source_target_pairs={{0,4},{1,3},{2,6},{3,1},{4,0},{5,7},{6,2},{7,5},{8,12},{9,11},{10,... | collective-permute-start | bytes 786440 | tf_op jit(solution)/shard_map/cond/branch_1_fun/ppermute | solution.py:241
  80.4 6.4 %collective-permute-start.14 = (bf16[2,128,512]{2,1,0:T(8,128)(2,1)S(1)}, bf16[2,128,512]{2,1,0:T(8,128)(2,1)S(1)}, u32[]{:S(2)}, u32[]{:S(2)}) collective-permute-start(bf16[2,128,512]{2,1,0:T(8,128)(2,1)S(1)} %collective-permute-done.13.refs_5_), channel_id=1, source_target_pairs={{0,4},{1,3},{2,6},{3,1},{4,0},{5,7},{6,2},{7,5},{8,12},{9,11},{10,... | collective-permute-start | bytes 786440 | tf_op jit(solution)/shard_map/cond/branch_1_fun/ppermute | solution.py:241
where the time goes:
time: 89 us; the launch traced here: 88.7 us
  waiting for transfers between devices  35 us (39%)
  starting transfers between devices  33.9 us (38%)
  Pallas kernels  15.9 us (18%)
  between operations  2.12 us (2%)
  local copies, waits for them, and re-layouts  0.94 us (1%)
    ppermute x10, waiting for transfers between devices, move(): return lax.ppermute(value, ('dp', 'expert'), pairs)  18.7 us
    ppermute x10, starting transfers between devices, move(): return lax.ppermute(value, ('dp', 'expert'), pairs)  11.5 us
    all_to_all x2, starting transfers between devices, body(): bids = lax.all_to_all(bids, everywhere, 0, 0, tiled=True)  9.79 us
    all_to_all x2, waiting for transfers between devices, body(): bids = lax.all_to_all(bids, everywhere, 0, 0, tiled=True)  8.72 us
    ppermute x4, starting transfers between devices, sent_on(): columns[k] = lax.ppermute(parcels[k], everywhere, pairs)  6.33 us
    all_to_all x1, waiting for transfers between devices, body(): info = lax.all_to_all(info, everywhere, 0, 0, tiled=True)  5.25 us
    pallas_call x3, Pallas kernels, write(): pl.pallas_call(functools.partial(assemble, plan), out_shape=jax.ShapeDtyp...  4.3 us
    pallas_call x1, Pallas kernels, body(): pl.pallas_call(functools.partial(opening, chunks), out_shape=[shape(rows,...  4.17 us
  transfers between devices with their start and end apart: 22, of which 12 were waited for; matrix products, arithmetic and copies ran while one was open for 0% of the time, Pallas kernels for 8%

commit v1 on v0

--- a/solution.py
+++ b/solution.py
@@ -63,8 +63,9 @@
     choice = jnp.min(jnp.where(values == top, ids, far), axis=1, keepdims=True)
     claims = ids == choice
     second = jnp.max(jnp.where(claims, lowest, values), axis=1, keepdims=True)
-    bids = jnp.where(claims, top - second + eps, -1.0)
-    return choice, claims, bids, jnp.max(bids, axis=0, keepdims=True)
+    bid = top - second + eps
+    bids = jnp.where(claims, bid, -1.0)
+    return choice, claims, bid, bids, jnp.max(bids, axis=0, keepdims=True)
 
 
 def first_round(place, kept, theirs, epsilon, values, out):
@@ -90,20 +91,19 @@
     out[...] = jnp.broadcast_to(raised[None], out.shape)
 
 
-def last_round(values, before, epsilon, bids, base, largest, out, after):
+def last_round(values, before, epsilon, bids, largest, out, after):
     rows, experts = values.shape
     total = before[...] + jnp.maximum(jnp.max(bids[...], axis=0), 0.0)
     after[...] = total
-    choice, claims, spread, raised = choose(values[...] - total, epsilon[0])
-    token = (base[0] + lax.broadcasted_iota(jnp.int32, (rows, experts), 0)).astype(jnp.float32)
-    first = jnp.min(jnp.where(claims & (spread == raised), token, far), axis=0, keepdims=True)
+    choice, claims, bid, _, _ = choose(values[...] - total, epsilon[0])
     count = jnp.sum(claims.astype(jnp.float32), axis=0, keepdims=True)
-    wide = out.shape[2] - 3 * experts
+    wide = (out.shape[2] - experts) // 2
     lane = lax.broadcasted_iota(jnp.int32, (rows, wide), 1)
-    row = lax.broadcasted_iota(jnp.int32, (rows, wide), 0)
-    turned = jnp.sum(jnp.where(lane == row, choice, 0.0), axis=0, keepdims=True)
-    turned = jnp.where(lane[:1] == rows, largest[:, :1], turned)
-    line = jnp.concatenate([raised, first, count, turned], axis=1)
+    same = lane == lax.broadcasted_iota(jnp.int32, (rows, wide), 0)
+    choices = jnp.sum(jnp.where(same, choice, 0.0), axis=0, keepdims=True)
+    choices = jnp.where(lane[:1] == rows, largest[:, :1], choices)
+    offered = jnp.sum(jnp.where(same, bid, 0.0), axis=0, keepdims=True)
+    line = jnp.concatenate([count, choices, offered], axis=1)
     out[...] = jnp.broadcast_to(line[None], out.shape)
 
 
@@ -128,21 +128,20 @@
     out[...] = value[...]
 
 
-def filled(line, value):
+def filled(line, value, flops):
     return pl.pallas_call(
         fill,
         out_shape=jax.ShapeDtypeStruct(value.shape, value.dtype),
         in_specs=[ANY, VMEM],
         out_specs=VMEM,
         compiler_params=room(4),
-        cost_estimate=pl.CostEstimate(flops=4000000000, bytes_accessed=4096, transcendentals=0),
+        cost_estimate=pl.CostEstimate(flops=flops, bytes_accessed=4096, transcendentals=0),
         name="filled",
     )(line, value)
 
 
-def add_up(ne, rows, top, place, info, columns, total_out, short_out):
+def add_up(ne, rows, top, at, place, info, columns, total_out, short_out):
     height = total_out.shape[0]
-    at = info.shape[2] // 128 * 128 - (rows // 128 + 1) * 128
     ids = place[0] + top + lax.broadcasted_iota(jnp.int32, (height, rows), 0)
     ids = ids.astype(jnp.float32)
     total = jnp.zeros(total_out.shape, jnp.float32)
@@ -157,40 +156,20 @@
     short_out[...] = total.astype(short_out.dtype)
 
 
-def more_sums(ne, rows, top, place, info, *refs):
-    add_up(ne, rows, top, place, info, refs[:-2], *refs[-2:])
-
-
-def finish(ne, rows, outer, place, info, before, prices, *refs):
-    columns, (final, holder, best, counts_out, fits, *sums) = refs[:-7], refs[-7:]
-    experts = before.shape[1]
-    own = prices.shape[1]
-    start = place[0]
-    if own % 128 == 0:
-        start = pl.multiple_of(start, 128)
-        raised = info[:, :, pl.ds(start, own)]
-        firsts = info[:, :, pl.ds(pl.multiple_of(experts + start, 128), own)]
-        earlier = before[:, pl.ds(start, own)]
-        top_bid = jnp.max(raised, axis=0)
-        first = jnp.min(jnp.where(raised == top_bid[None], firsts, far), axis=0)
-        final[...] = prices[...] + earlier + jnp.maximum(top_bid, 0.0)
-        holder[...] = jnp.where(top_bid > 0, first, -1.0).astype(jnp.int32)
-    else:
-        raised = info[:, :, :experts]
-        top_bid = jnp.max(raised, axis=0)
-        firsts = jnp.where(raised == top_bid[None], info[:, :, experts : 2 * experts], far)
-        final[...] = before[...] + jnp.maximum(top_bid, 0.0)
-        holder[...] = jnp.where(top_bid > 0, jnp.min(firsts, axis=0), -1.0).astype(jnp.int32)
-    at = 3 * experts
-    for c in range(ne):
-        mark = info[place[1] * ne + c, :, at : at + rows]
+def more_sums(ne, rows, top, at, place, info, *refs):
+    add_up(ne, rows, top, at, place, info, refs[:-2], *refs[-2:])
+
+
+def finish(ne, rows, outer, experts, place, info, *refs):
+    columns, (best, counts_out, fits, *sums) = refs[:-6], refs[-5:]
+    own = counts_out.shape[0]
+    marks = [info[place[1] * ne + c, :, experts : experts + rows] for c in range(ne)]
+    for c, mark in enumerate(marks):
         best[:, c * rows : (c + 1) * rows] = mark.astype(jnp.int32)
-    add_up(ne, rows, 0, place, info, columns, *sums)
+    add_up(ne, rows, 0, experts, place, info, columns, *sums)
     share = info.shape[0] // outer
-    each = [
-        jnp.sum(info[i * share : (i + 1) * share, :, 2 * experts : at], axis=0) for i in range(outer)
-    ]
-    largest = jnp.max(info[:, :, at + rows : at + rows + 1])
+    each = [jnp.sum(info[i * share : (i + 1) * share, :, :experts], axis=0) for i in range(outer)]
+    largest = jnp.max(info[:, :, experts + rows : experts + rows + 1])
     fullest = jnp.max(functools.reduce(jnp.maximum, each))
     fits[0] = jnp.where(fullest * largest <= 256.0, 1, 0)
     counts = functools.reduce(jnp.add, each)
@@ -198,6 +177,42 @@
     lane = lax.broadcasted_iota(jnp.int32, (own, experts), 1)
     counts = jnp.sum(jnp.where(expert_row == lane, counts, 0.0), axis=1, keepdims=True)
     counts_out[...] = jnp.broadcast_to(jnp.maximum(counts, 1.0), counts_out.shape)
+
+
+def settle(rows, experts, place, info, before, prices, final, holder):
+    own = prices.shape[1]
+    wide = (info.shape[2] - experts) // 2
+    devices = info.shape[0]
+    ids = (place[0] + lax.broadcasted_iota(jnp.int32, (own, rows), 0)).astype(jnp.float32)
+    offset = lax.broadcasted_iota(jnp.int32, (own, rows), 1).astype(jnp.float32)
+
+    def claimed(n):
+        return ids == info[n, :, experts : experts + rows]
+
+    def offered(n):
+        return info[n, :, experts + wide : experts + wide + rows]
+
+    def higher(n, top):
+        return jnp.maximum(top, jnp.where(claimed(n), offered(n), -1.0))
+
+    top = lax.fori_loop(0, devices, higher, jnp.full((own, rows), -1.0, jnp.float32))
+    top = jnp.max(top, axis=1, keepdims=True)
+
+    def earlier(n, first):
+        token = (n * rows).astype(jnp.float32) + offset
+        return jnp.minimum(first, jnp.where(claimed(n) & (offered(n) == top), token, far))
+
+    first = lax.fori_loop(0, devices, earlier, jnp.full((own, rows), far, jnp.float32))
+    first = jnp.min(first, axis=1, keepdims=True)
+    same = lax.broadcasted_iota(jnp.int32, (own, own), 0) == lax.broadcasted_iota(jnp.int32, (own, own), 1)
+    raised = jnp.sum(jnp.where(same, jnp.maximum(top, 0.0), 0.0), axis=0, keepdims=True)
+    held = jnp.sum(jnp.where(same, jnp.where(top > 0, first, -1.0), 0.0), axis=0, keepdims=True)
+    expert_row = place[0] + lax.broadcasted_iota(jnp.int32, (own, experts), 0)
+    lane = lax.broadcasted_iota(jnp.int32, (own, experts), 1)
+    so_far = jnp.sum(jnp.where(expert_row == lane, before[...], 0.0), axis=1, keepdims=True)
+    so_far = jnp.sum(jnp.where(same, so_far, 0.0), axis=0, keepdims=True)
+    final[...] = prices[...] + so_far + raised
+    holder[...] = held.astype(jnp.int32)
 
 
 def blend(row, centroids, counts, *refs):
@@ -275,7 +290,11 @@
             if stage < bits - 1 or stage < 2:
                 held[p].append(onward(held[p]))
             else:
-                late[p] = [onward(held[p][:-1]), onward(held[p][-1:])]
+                early = onward(held[p][:-1])
+                value, where = held[p][-1]
+                value, sent = lax.optimization_barrier((value, early[0]))
+                held[p][-1] = (value, where)
+                late[p] = [(sent, early[1]), onward(held[p][-1:])]
     def write(whole, groups):
         pieces, plan, slots = [], [], []
         for p, group in enumerate(groups):
@@ -404,49 +423,57 @@
         sent_on(k)
     bids = lax.all_to_all(bids, everywhere, 0, 0, tiled=True)
     wide = (rows // 128 + 1) * 128
-    largest = filled(total, largest)
-    base = (dp_at * local_tokens + expert_at * rows).astype(jnp.int32).reshape(1)
+    largest = filled(total, largest, 8000000000)
     info, total = pl.pallas_call(
         last_round,
-        out_shape=(shape(devices, 1, 3 * experts + wide), line),
-        in_specs=[VMEM, VMEM, SMEM, VMEM, SMEM, VMEM],
+        out_shape=(shape(devices, 1, experts + 2 * wide), line),
+        in_specs=[VMEM, VMEM, SMEM, VMEM, VMEM],
         out_specs=(VMEM, VMEM),
         compiler_params=room(8),
         name="last_round",
-    )(values, total, epsilon, bids, base, largest)
+    )(values, total, epsilon, bids, largest)
     if paired:
         columns += [lax.ppermute(c, "expert", swap) for c in columns]
     info = lax.all_to_all(info, everywhere, 0, 0, tiled=True)
 
+    timed = filled(total, largest, 8000000000)
     place = jnp.stack([expert_at * own, dp_at] + sources).astype(jnp.int32)
-    direct = own % 128 == 0
-    listed = own if direct else experts
     low = own // 32 * 16 if own % 32 == 0 else own
     heights = [low, own - low] if paired else [own]
 
     def two(height):
         return (shape(height, cols), shape(height, cols, dtype=jnp.bfloat16))
 
-    final, holder, best, counts, fits, *sums = pl.pallas_call(
-        functools.partial(finish, ne, rows, outer),
+    best, counts, fits, *sums = pl.pallas_call(
+        functools.partial(finish, ne, rows, outer, experts),
         out_shape=(
-            shape(1, listed),
-            shape(1, listed, dtype=jnp.int32),
             shape(1, local_tokens, dtype=jnp.int32),
             shape(own, 128),
             shape(1, dtype=jnp.int32),
         )
         + two(heights[0]),
-        in_specs=[SMEM] + [VMEM] * (3 + len(columns)),
-        out_specs=(VMEM, VMEM, VMEM, VMEM, SMEM, VMEM, VMEM),
+        in_specs=[SMEM] + [VMEM] * (1 + len(columns)) + [ANY],
+        out_specs=(VMEM, VMEM, SMEM, VMEM, VMEM),
         compiler_params=room(16),
         name="finish",
-    )(place, info, total, prices.reshape(1, own), *columns)
+    )(place, info, *columns, timed)
+
+    def settled(place, info, total, prices):
+        return pl.pallas_call(
+            functools.partial(settle, rows, experts),
+            out_shape=(shape(1, own), shape(1, own, dtype=jnp.int32)),
+            in_specs=[SMEM, VMEM, VMEM, VMEM],
+            out_specs=(VMEM, VMEM),
+            compiler_params=room(16),
+            name="settle",
+        )(place, info, total, prices)
+
+    prices = prices.reshape(1, own)
     if paired:
 
-        def rest(wide, place, info, columns, sums, best, mine, counts):
+        def rest(wide, place, info, total, prices, columns, sums, mine, counts):
             more = pl.pallas_call(
-                functools.partial(more_sums, ne, rows, heights[0]),
+                functools.partial(more_sums, ne, rows, heights[0], experts),
                 out_shape=two(heights[1]),
                 in_specs=[SMEM] + [VMEM] * (1 + len(columns)),
                 out_specs=(VMEM, VMEM),
@@ -455,23 +482,18 @@
             )(place, info, *columns)
             pairs = list(zip(sums, more))
             whole = spread_out(dp, inner, wide, pairs[0], pairs[1], mine, counts)
-            return best[0], whole
-
-        best, refreshed = lax.switch(
+            return *settled(place, info, total, prices), whole
+
+        final, holder, refreshed = lax.switch(
             fits[0],
             [functools.partial(rest, True), functools.partial(rest, False)],
-            place, info, columns, sums, best, mine, counts,
+            place, info, total, prices, columns, sums, mine, counts,
         )
     else:
-        best = best[0]
+        final, holder = settled(place, info, total, prices)
         fresh = 0.5 * mine.astype(f32) + 0.5 * sums[0] / counts[:, :1]
         refreshed = lax.all_gather(fresh.astype(centroids.dtype), "dp", axis=1, tiled=True)
-    if direct:
-        final, holder = final[0], holder[0]
-    else:
-        final = prices + lax.dynamic_slice_in_dim(final[0], expert_at * own, own, 0)
-        holder = lax.dynamic_slice_in_dim(holder[0], expert_at * own, own, 0)
-    return final, best, holder, refreshed
+    return final[0], best[0], holder[0], refreshed
 
 
 def solution(mesh):

time: 89 us -> 103 us (1.16)
  Pallas kernels: 15.9 us -> 22.1 us
  starting transfers between devices: 33.9 us -> 39.2 us
  waiting for transfers between devices: 35 us -> 38 us
    ppermute x10, waiting for transfers between devices: 18.7 us -> 24.9 us  [move(): return lax.ppermute(value, ('dp', 'expert'), pairs)]
    pallas_call x3 -> x4, Pallas kernels: 5.31 us -> 11.4 us  [the longest x1 5.53 us: settled(): pl.pallas_call(functools.partial(settle, rows, experts), out_shape=(shape...]
    ppermute x10, starting transfers between devices: 11.5 us -> 15 us  [move(): return lax.ppermute(value, ('dp', 'expert'), pairs)]
    all_to_all x2, waiting for transfers between devices: 8.72 us -> 6.02 us  [body(): bids = lax.all_to_all(bids, everywhere, 0, 0, tiled=True)]
    ppermute x4, starting transfers between devices: 3.22 us -> 4.48 us  [body(): columns += [lax.ppermute(c, 'expert', swap) for c in columns]]
  transfers between devices with their start and end apart: 22 -> 22, of which waited for: 12 -> 11; matrix products, arithmetic and copies ran while one was open for 0% -> 0% of each run, Pallas kernels for 8% -> 13%
where the time goes in v1:
time: 103 us
  starting transfers between devices  39.2 us (38%)
  waiting for transfers between devices  38 us (37%)
  Pallas kernels  22.1 us (21%)
  between operations  2.12 us (2%)
    ppermute x10, waiting for transfers between devices, move(): return lax.ppermute(value, ('dp', 'expert'), pairs)  24.9 us
    ppermute x10, starting transfers between devices, move(): return lax.ppermute(value, ('dp', 'expert'), pairs)  15 us
    all_to_all x2, starting transfers between devices, body(): bids = lax.all_to_all(bids, everywhere, 0, 0, tiled=True)  9.79 us
    ppermute x4, starting transfers between devices, sent_on(): columns[k] = lax.ppermute(parcels[k], everywhere, pairs)  6.34 us
    all_to_all x2, waiting for transfers between devices, body(): bids = lax.all_to_all(bids, everywhere, 0, 0, tiled=True)  6.02 us
    pallas_call x1, Pallas kernels, settled(): pl.pallas_call(functools.partial(settle, rows, experts), out_shape=(shape...  5.53 us
    all_to_all x1, waiting for transfers between devices, body(): info = lax.all_to_all(info, everywhere, 0, 0, tiled=True)  4.72 us
    ppermute x4, starting transfers between devices, body(): columns += [lax.ppermute(c, 'expert', swap) for c in columns]  4.48 us
  transfers between devices with their start and end apart: 22, of which 11 were waited for; matrix products, arithmetic and copies ran while one was open for 0% of the time, Pallas kernels for 13%

profile of v1, /device:TPU:0, one launch (start us, length us, event | category | flops | bytes accessed | tf_op | source)
XLA Modules:
  0.0 102.6 jit_solution(17265196725135824548)
XLA Ops:
  0.7 0.1 stack.182.place
  0.8 4.3 %opening.1 = (f32[192,256]{1,0:T(8,128)S(1)}, f32[192,256]{1,0:T(8,128)S(1)}, bf16[256,512]{1,0:T(8,128)(2,1)S(1)}, f32[1,128]{1,0:T(1,128)S(1)}, bf16[384,512]{...) custom-call(s32[7]{0:T(128)S(1)} %stack.182.place, ...), custom_call_target="tpu_custom_call" | custom-call | tf_op jit(solution)/shard_map/opening/pallas_call | solution.py:353
  5.1 0.5 collective-permute-start.20
  6.3 0.4 collective-permute-done.20.theirs
  6.7 0.9 first_round.1
  7.7 7.2 %all-to-all-start = ((f32[32,1,512]{2,1,0:T(1,128)}), f32[32,1,512]{2,1,0:T(1,128)S(1)}, u32[]{:S(2)}, u32[]{:S(2)}) async-start(f32[32,1,512]{2,1,0:T(1,128)} %get-tuple-element.139), calls=%async_computation | async-start | bytes 131072 | tf_op jit(solution)/shard_map/all_to_all | solution.py:411
  14.9 1.8 %collective-permute-start.23 = (bf16[384,512]{1,0:T(8,128)(2,1)S(1)}, bf16[384,512]{1,0:T(8,128)(2,1)S(1)}, u32[]{:S(2)}, u32[]{:S(2)}) collective-permute-start(bf16[384,512]{1,0:T(8,128)(2,1)S(1)} %get-tuple-element.148), channel_id=1, source_target_pairs={{0,4},{1,11},{2,6},{3,9},{4,0},{5,15},{6,2},{7,13},{8,12},{9,3},{1... | collective-permute-start | bytes 1179656 | tf_op jit(solution)/shard_map/ppermute | solution.py:382
  16.7 1.5 %collective-permute-start.24 = (bf16[384,512]{1,0:T(8,128)(2,1)S(1)}, bf16[384,512]{1,0:T(8,128)(2,1)S(1)}, u32[]{:S(2)}, u32[]{:S(2)}) collective-permute-start(bf16[384,512]{1,0:T(8,128)(2,1)S(1)} %get-tuple-element.149), channel_id=1, source_target_pairs={{0,6},{1,9},{2,4},{3,11},{4,2},{5,13},{6,0},{7,15},{8,14},{9,1},{1... | collective-permute-start | bytes 1179656 | tf_op jit(solution)/shard_map/ppermute | solution.py:382
  18.2 0.1 stack.174.place
  18.3 4.3 %all-to-all-done.bids = f32[32,1,512]{2,1,0:T(1,128)S(1)} async-done(((f32[32,1,512]{2,1,0:T(1,128)}), f32[32,1,512]{2,1,0:T(1,128)S(1)}, u32[]{:S(2)}, u32[]{:S(2)}) %all-to-all-start) | async-done | bytes 65568 | tf_op jit(solution)/shard_map/all_to_all | solution.py:411
  22.6 0.9 next_round.1
  23.5 2.6 %all-to-all-start.1 = ((f32[32,1,512]{2,1,0:T(1,128)}), f32[32,1,512]{2,1,0:T(1,128)S(1)}, u32[]{:S(2)}, u32[]{:S(2)}) async-start(f32[32,1,512]{2,1,0:T(1,128)} %get-tuple-element.141), calls=%async_computation.1 | async-start | bytes 131072 | tf_op jit(solution)/shard_map/all_to_all | solution.py:424
  26.1 1.4 %collective-permute-start.21 = (bf16[384,512]{1,0:T(8,128)(2,1)S(1)}, bf16[384,512]{1,0:T(8,128)(2,1)}, u32[]{:S(2)}, u32[]{:S(2)}) collective-permute-start(bf16[384,512]{1,0:T(8,128)(2,1)S(1)} %get-tuple-element.146), channel_id=1, source_target_pairs={{0,0},{1,15},{2,2},{3,13},{4,4},{5,11},{6,6},{7,9},{8,8},{9,7},{10... | collective-permute-start | bytes 1179656 | tf_op jit(solution)/shard_map/ppermute | solution.py:382
  27.5 1.6 %collective-permute-start.22 = (bf16[384,512]{1,0:T(8,128)(2,1)S(1)}, bf16[384,512]{1,0:T(8,128)(2,1)}, u32[]{:S(2)}, u32[]{:S(2)}) collective-permute-start(bf16[384,512]{1,0:T(8,128)(2,1)S(1)} %get-tuple-element.147), channel_id=1, source_target_pairs={{0,2},{1,13},{2,0},{3,15},{4,6},{5,9},{6,4},{7,11},{8,10},{9,5},{1... | collective-permute-start | bytes 1179656 | tf_op jit(solution)/shard_map/ppermute | solution.py:382
  29.1 2.5 %collective-permute-start.27 = (bf16[384,512]{1,0:T(8,128)(2,1)S(1)}, bf16[384,512]{1,0:T(8,128)(2,1)S(1)}, u32[]{:S(2)}, u32[]{:S(2)}) collective-permute-start(bf16[384,512]{1,0:T(8,128)(2,1)S(1)} %collective-permute-done.23.refs_2_), channel_id=1, source_target_pairs={{0,1},{1,0},{2,3},{3,2},{4,5},{5,4},{6,7},{7,6},{8,9},{9,8},{10,11... | collective-permute-start | bytes 1179656 | tf_op jit(solution)/shard_map/ppermute | solution.py:436
  31.7 1.8 %all-to-all-done.1.bids = f32[32,1,512]{2,1,0:T(1,128)S(1)} async-done(((f32[32,1,512]{2,1,0:T(1,128)}), f32[32,1,512]{2,1,0:T(1,128)S(1)}, u32[]{:S(2)}, u32[]{:S(2)}) %all-to-all-start.1) | async-done | bytes 65568 | tf_op jit(solution)/shard_map/all_to_all | solution.py:424
  33.5 1.0 last_round.1
  34.5 3.1 %all-to-all-start.2 = ((f32[32,1,1024]{2,1,0:T(1,128)}), f32[32,1,1024]{2,1,0:T(1,128)S(1)}, u32[]{:S(2)}, u32[]{:S(2)}) async-start(f32[32,1,1024]{2,1,0:T(1,128)} %get-tuple-element.143), calls=%async_computation.2 | async-start | bytes 262144 | tf_op jit(solution)/shard_map/all_to_all | solution.py:437
  37.6 0.3 collective-permute-start.25
  37.9 2.0 %collective-permute-done.22.refs_1_ = bf16[384,512]{1,0:T(8,128)(2,1)} collective-permute-done((bf16[384,512]{1,0:T(8,128)(2,1)S(1)}, bf16[384,512]{1,0:T(8,128)(2,1)}, u32[]{:S(2)}, u32[]{:S(2)}) %collective-permute-start.22) | collective-permute-done | bytes 393248 | tf_op jit(solution)/shard_map/ppermute | solution.py:382
  39.9 1.6 %collective-permute-start.26 = (bf16[384,512]{1,0:T(8,128)(2,1)}, bf16[384,512]{1,0:T(8,128)(2,1)S(1)}, u32[]{:S(2)}, u32[]{:S(2)}) collective-permute-start(bf16[384,512]{1,0:T(8,128)(2,1)} %collective-permute-done.22.refs_1_), channel_id=1, source_target_pairs={{0,1},{1,0},{2,3},{3,2},{4,5},{5,4},{6,7},{7,6},{8,9},{9,8},{10,11... | collective-permute-start | bytes 1179656 | tf_op jit(solution)/shard_map/ppermute | solution.py:436
  41.4 4.7 %all-to-all-done.2.info = f32[32,1,1024]{2,1,0:T(1,128)S(1)} async-done(((f32[32,1,1024]{2,1,0:T(1,128)}), f32[32,1,1024]{2,1,0:T(1,128)S(1)}, u32[]{:S(2)}, u32[]{:S(2)}) %all-to-all-start.2) | async-done | bytes 131104 | tf_op jit(solution)/shard_map/all_to_all | solution.py:437
  46.2 2.4 %finish.1 = (s32[1,384]{1,0:T(1,128)S(1)}, f32[256,128]{1,0:T(8,128)S(1)}, s32[1]{0:T(128)}, f32[128,512]{1,0:T(8,128)S(1)}, bf16[128,512]{1,0:T(8,128)(2,1)S(1)}) custom-call(s32[10]{0:T(128)S(1)} %stack.174.place, f32[32,1,1024]{2,1,0:T(1,128)S(1)} %all-to-all-done.2.info, bf16[384,512]{1,0:T(8,128)(2,1)} %collective-permute-done.21.refs_0_, ...), custom_call_target="tpu_custom_call" | custom-call | tf_op jit(solution)/shard_map/finish/pallas_call | solution.py:447
  48.5 0.6 reduce
  49.8 52.8 %conditional.1 = (f32[1,256]{1,0:T(1,128)}, s32[1,256]{1,0:T(1,128)}, bf16[256,4096]{1,0:T(8,128)(2,1)}) conditional(s32[]{:T(128)} %bitcast.50, (s32[10]{0:T(128)S(1)}, f32[32,1,1024]{2,1,0:T(1,128)S(1)}, f32[1,512]{1,0:T(1,128)S(1)}, f32[1,256]{1,0:T(1,128)S(1)}, bf16[384,512]{1,0:T(8,128)(2,1)}, /*index=5*/bf16[384,512]{1,0:T(8,128)(2,1)}, ...), branch_computations={%region_0.1_spmd, %region_1.2_spmd} | conditional | flops 262210 | bytes 10486794 | solution.py:487
  49.8 0.8 collective-permute-start.5
  50.6 2.5 %more_sums.2 = (f32[128,512]{1,0:T(8,128)S(1)}, bf16[128,512]{1,0:T(8,128)(2,1)}) custom-call(s32[10]{0:T(128)S(1)} %get-tuple-element.62.place, f32[32,1,1024]{2,1,0:T(1,128)S(1)} %get-tuple-element.63.info, bf16[384,512]{1,0:T(8,128)(2,1)} %get-tuple-element.70.refs_0_, bf16[384,512]{1,0:T(8,128)(2,1)} %get-tuple-element.71.refs_1_, ...), custom_call_target="tpu_custom_call" | custom-call | tf_op jit(solution)/shard_map/cond/branch_0_fun/more_sums/pallas_call | solution.py:475
  53.1 2.1 %collective-permute-start = (f32[128,512]{1,0:T(8,128)S(1)}, f32[128,512]{1,0:T(8,128)S(1)}, u32[]{:S(2)}, u32[]{:S(2)}) collective-permute-start(f32[128,512]{1,0:T(8,128)S(1)} %get-tuple-element.78.refs_0_), channel_id=1, source_target_pairs={{0,16},{1,17},{2,18},{3,19},{4,20},{5,21},{6,22},{7,23},{8,24},{9,... | collective-permute-start | bytes 786440 | tf_op jit(solution)/shard_map/cond/branch_0_fun/ppermute | solution.py:256
  55.3 14.6 %collective-permute-done.5.refs_1_ = f32[128,512]{1,0:T(8,128)S(1)} collective-permute-done((f32[128,512]{1,0:T(8,128)S(1)}, f32[128,512]{1,0:T(8,128)S(1)}, u32[]{:S(2)}, u32[]{:S(2)}) %collective-permute-start.5) | collective-permute-done | bytes 262176 | tf_op jit(solution)/shard_map/cond/branch_0_fun/ppermute | solution.py:256
  69.8 0.1 blend.5
  69.9 1.5 %collective-permute-start.6 = (bf16[1,128,512]{2,1,0:T(8,128)(2,1)S(1)}, bf16[1,128,512]{2,1,0:T(8,128)(2,1)S(1)}, u32[]{:S(2)}, u32[]{:S(2)}) collective-permute-start(bf16[1,128,512]{2,1,0:T(8,128)(2,1)S(1)} %bitcast.59), channel_id=1, source_target_pairs={{0,2},{1,5},{2,0},{3,7},{4,6},{5,1},{6,4},{7,3},{8,10},{9,13},{10,... | collective-permute-start | bytes 393224 | tf_op jit(solution)/shard_map/cond/branch_0_fun/ppermute | solution.py:256
  71.5 3.9 %collective-permute-done.refs_1_ = f32[128,512]{1,0:T(8,128)S(1)} collective-permute-done((f32[128,512]{1,0:T(8,128)S(1)}, f32[128,512]{1,0:T(8,128)S(1)}, u32[]{:S(2)}, u32[]{:S(2)}) %collective-permute-start) | collective-permute-done | bytes 262176 | tf_op jit(solution)/shard_map/cond/branch_0_fun/ppermute | solution.py:256
  75.3 0.1 blend.4
  75.6 1.7 %collective-permute-start.7 = (bf16[2,128,512]{2,1,0:T(8,128)(2,1)S(1)}, bf16[2,128,512]{2,1,0:T(8,128)(2,1)S(1)}, u32[]{:S(2)}, u32[]{:S(2)}) collective-permute-start(bf16[2,128,512]{2,1,0:T(8,128)(2,1)S(1)} %pad_maximum_fusion.1), channel_id=1, source_target_pairs={{0,4},{1,9},{2,6},{3,11},{4,0},{5,13},{6,2},{7,15},{8,12},{9,1},{1... | collective-permute-start | bytes 786440 | tf_op jit(solution)/shard_map/cond/branch_0_fun/ppermute | solution.py:256
  77.3 2.0 %collective-permute-start.8 = (bf16[2,128,512]{2,1,0:T(8,128)(2,1)S(1)}, bf16[2,128,512]{2,1,0:T(8,128)(2,1)S(1)}, u32[]{:S(2)}, u32[]{:S(2)}) collective-permute-start(bf16[2,128,512]{2,1,0:T(8,128)(2,1)S(1)} %pad_maximum_fusion.1), channel_id=1, source_target_pairs={{0,8},{1,3},{2,10},{3,1},{4,12},{5,7},{6,14},{7,5},{8,0},{9,11},{1... | collective-permute-start | bytes 786440 | tf_op jit(solution)/shard_map/cond/branch_0_fun/ppermute | solution.py:256
  79.3 2.2 %collective-permute-done.1.refs_4_ = bf16[1,128,512]{2,1,0:T(8,128)(2,1)S(1)} collective-permute-done((bf16[1,128,512]{2,1,0:T(8,128)(2,1)S(1)}, bf16[1,128,512]{2,1,0:T(8,128)(2,1)S(1)}, u32[]{:S(2)}, u32[]{:S(2)}) %collective-permute-start.1) | collective-permute-done | bytes 131104 | tf_op jit(solution)/shard_map/cond/branch_0_fun/ppermute | solution.py:256
  81.6 1.5 %collective-permute-start.2 = (bf16[2,128,512]{2,1,0:T(8,128)(2,1)S(1)}, bf16[2,128,512]{2,1,0:T(8,128)(2,1)S(1)}, u32[]{:S(2)}, u32[]{:S(2)}) collective-permute-start(bf16[2,128,512]{2,1,0:T(8,128)(2,1)S(1)} %pad_maximum_fusion), channel_id=1, source_target_pairs={{0,2},{1,9},{2,0},{3,11},{4,6},{5,13},{6,4},{7,15},{8,10},{9,1},{1... | collective-permute-start | bytes 786440 | tf_op jit(solution)/shard_map/cond/branch_0_fun/ppermute | solution.py:256
  83.1 0.8 collective-permute-start.3
  83.8 3.4 %collective-permute-done.8.refs_0_ = bf16[2,128,512]{2,1,0:T(8,128)(2,1)S(1)} collective-permute-done((bf16[2,128,512]{2,1,0:T(8,128)(2,1)S(1)}, bf16[2,128,512]{2,1,0:T(8,128)(2,1)S(1)}, u32[]{:S(2)}, u32[]{:S(2)}) %collective-permute-start.8) | collective-permute-done | bytes 262176 | tf_op jit(solution)/shard_map/cond/branch_0_fun/ppermute | solution.py:256
  87.2 1.4 %collective-permute-start.9 = (bf16[2,128,512]{2,1,0:T(8,128)(2,1)S(1)}, bf16[2,128,512]{2,1,0:T(8,128)(2,1)S(1)}, u32[]{:S(2)}, u32[]{:S(2)}) collective-permute-start(bf16[2,128,512]{2,1,0:T(8,128)(2,1)S(1)} %collective-permute-done.7.refs_2_), channel_id=1, source_target_pairs={{0,8},{1,3},{2,10},{3,1},{4,12},{5,7},{6,14},{7,5},{8,0},{9,11},{1... | collective-permute-start | bytes 786440 | tf_op jit(solution)/shard_map/cond/branch_0_fun/ppermute | solution.py:256
  88.6 0.3 collective-permute-done.2.refs_5_
  88.9 0.5 collective-permute-done.3.refs_0_
  89.4 3.0 %collective-permute-start.4 = (bf16[2,128,512]{2,1,0:T(8,128)(2,1)S(1)}, bf16[2,128,512]{2,1,0:T(8,128)(2,1)S(1)}, u32[]{:S(2)}, u32[]{:S(2)}) collective-permute-start(bf16[2,128,512]{2,1,0:T(8,128)(2,1)S(1)} %collective-permute-done.2.refs_5_), channel_id=1, source_target_pairs={{0,4},{1,3},{2,6},{3,1},{4,0},{5,7},{6,2},{7,5},{8,12},{9,11},{10,... | collective-permute-start | bytes 786440 | tf_op jit(solution)/shard_map/cond/branch_0_fun/ppermute | solution.py:256
  92.5 5.5 %settle.2 = (f32[1,256]{1,0:T(1,128)}, s32[1,256]{1,0:T(1,128)}) custom-call(s32[10]{0:T(128)S(1)} %get-tuple-element.62.place, f32[32,1,1024]{2,1,0:T(1,128)S(1)} %get-tuple-element.63.info, f32[1,512]{1,0:T(1,128)S(1)} %get-tuple-element.64.before, f32[1,256]{1,0:T(1,128)S(1)} %get-tuple-element.65.prices), custom_call_target="tpu_custom_call" | custom-call | tf_op jit(solution)/shard_map/cond/branch_0_fun/settle/pallas_call | solution.py:462
  98.0 0.1 stack.127.base
  98.2 1.6 %assemble.6.refs_2_ = bf16[256,4096]{1,0:T(8,128)(2,1)} custom-call(s32[8]{0:T(128)S(1)} %stack.127.base, bf16[1,128,512]{2,1,0:T(8,128)(2,1)S(1)} %bitcast.61, bf16[1,128,512]{2,1,0:T(8,128)(2,1)S(1)} %collective-permute-done.6.refs_1_, bf16[2,128,512]{2,1,0:T(8,128)(2,1)S(1)} %collective-permute-done.7.refs_2_, bf16[1,128,512]{2,1,0:T(8,128)(2,1)S(1)} %bitcast.64, ...), custom_call_target="tpu_custom_call" | custom-call | tf_op jit(solution)/shard_map/cond/branch_0_fun/assemble/pallas_call | solution.py:307
  99.8 1.4 %assemble.7.refs_2_ = bf16[256,4096]{1,0:T(8,128)(2,1)} custom-call(s32[4]{0:T(128)S(1)} %add_add_fusion.1.base, bf16[2,128,512]{2,1,0:T(8,128)(2,1)S(1)} %collective-permute-done.8.refs_0_, bf16[2,128,512]{2,1,0:T(8,128)(2,1)S(1)} %collective-permute-done.9.refs_1_, bf16[256,4096]{1,0:T(8,128)(2,1)} %assemble.6.refs_2_), custom_call_target="tpu_custom_call", output_to_operand_aliasing={{}: (3, {})} | custom-call | tf_op jit(solution)/shard_map/cond/branch_0_fun/assemble/pallas_call | solution.py:307
  101.2 1.4 %assemble.8 = bf16[256,4096]{1,0:T(8,128)(2,1)} custom-call(s32[4]{0:T(128)S(1)} %add_add_fusion.base, bf16[2,128,512]{2,1,0:T(8,128)(2,1)S(1)} %collective-permute-done.3.refs_0_, bf16[2,128,512]{2,1,0:T(8,128)(2,1)S(1)} %collective-permute-done.4.refs_1_, bf16[256,4096]{1,0:T(8,128)(2,1)} %assemble.7.refs_2_), custom_call_target="tpu_custom_call", output_to_operand_aliasing={{}: (3, {})} | custom-call | tf_op jit(solution)/shard_map/cond/branch_0_fun/assemble/pallas_call | solution.py:307
  (23 shorter events, 0.4 us)
Async XLA Ops:
  5.1 1.6 %collective-permute-start.20 = (f32[192,256]{1,0:T(8,128)S(1)}, f32[192,256]{1,0:T(8,128)S(1)}, u32[]{:S(2)}, u32[]{:S(2)}) collective-permute-start(f32[192,256]{1,0:T(8,128)S(1)} %get-tuple-element.137), channel_id=1, source_target_pairs={{0,1},{1,0},{2,3},{3,2},{4,5},{5,4},{6,7},{7,6},{8,9},{9,8},{10,11... | collective-permute-start | bytes 589832 | tf_op jit(solution)/shard_map/ppermute | solution.py:369
  7.7 14.9 %all-to-all-start = ((f32[32,1,512]{2,1,0:T(1,128)}), f32[32,1,512]{2,1,0:T(1,128)S(1)}, u32[]{:S(2)}, u32[]{:S(2)}) async-start(f32[32,1,512]{2,1,0:T(1,128)} %get-tuple-element.139), calls=%async_computation | async-start | bytes 131072 | tf_op jit(solution)/shard_map/all_to_all | solution.py:411
  14.9 14.2 %collective-permute-start.23 = (bf16[384,512]{1,0:T(8,128)(2,1)S(1)}, bf16[384,512]{1,0:T(8,128)(2,1)S(1)}, u32[]{:S(2)}, u32[]{:S(2)}) collective-permute-start(bf16[384,512]{1,0:T(8,128)(2,1)S(1)} %get-tuple-element.148), channel_id=1, source_target_pairs={{0,4},{1,11},{2,6},{3,9},{4,0},{5,15},{6,2},{7,13},{8,12},{9,3},{1... | collective-permute-start | bytes 1179656 | tf_op jit(solution)/shard_map/ppermute | solution.py:382
  16.7 14.9 %collective-permute-start.24 = (bf16[384,512]{1,0:T(8,128)(2,1)S(1)}, bf16[384,512]{1,0:T(8,128)(2,1)S(1)}, u32[]{:S(2)}, u32[]{:S(2)}) collective-permute-start(bf16[384,512]{1,0:T(8,128)(2,1)S(1)} %get-tuple-element.149), channel_id=1, source_target_pairs={{0,6},{1,9},{2,4},{3,11},{4,2},{5,13},{6,0},{7,15},{8,14},{9,1},{1... | collective-permute-start | bytes 1179656 | tf_op jit(solution)/shard_map/ppermute | solution.py:382
  23.5 10.0 %all-to-all-start.1 = ((f32[32,1,512]{2,1,0:T(1,128)}), f32[32,1,512]{2,1,0:T(1,128)S(1)}, u32[]{:S(2)}, u32[]{:S(2)}) async-start(f32[32,1,512]{2,1,0:T(1,128)} %get-tuple-element.141), calls=%async_computation.1 | async-start | bytes 131072 | tf_op jit(solution)/shard_map/all_to_all | solution.py:424
  26.1 11.5 %collective-permute-start.21 = (bf16[384,512]{1,0:T(8,128)(2,1)S(1)}, bf16[384,512]{1,0:T(8,128)(2,1)}, u32[]{:S(2)}, u32[]{:S(2)}) collective-permute-start(bf16[384,512]{1,0:T(8,128)(2,1)S(1)} %get-tuple-element.146), channel_id=1, source_target_pairs={{0,0},{1,15},{2,2},{3,13},{4,4},{5,11},{6,6},{7,9},{8,8},{9,7},{10... | collective-permute-start | bytes 1179656 | tf_op jit(solution)/shard_map/ppermute | solution.py:382
  27.5 12.4 %collective-permute-start.22 = (bf16[384,512]{1,0:T(8,128)(2,1)S(1)}, bf16[384,512]{1,0:T(8,128)(2,1)}, u32[]{:S(2)}, u32[]{:S(2)}) collective-permute-start(bf16[384,512]{1,0:T(8,128)(2,1)S(1)} %get-tuple-element.147), channel_id=1, source_target_pairs={{0,2},{1,13},{2,0},{3,15},{4,6},{5,9},{6,4},{7,11},{8,10},{9,5},{1... | collective-permute-start | bytes 1179656 | tf_op jit(solution)/shard_map/ppermute | solution.py:382
  29.1 17.0 %collective-permute-start.27 = (bf16[384,512]{1,0:T(8,128)(2,1)S(1)}, bf16[384,512]{1,0:T(8,128)(2,1)S(1)}, u32[]{:S(2)}, u32[]{:S(2)}) collective-permute-start(bf16[384,512]{1,0:T(8,128)(2,1)S(1)} %collective-permute-done.23.refs_2_), channel_id=1, source_target_pairs={{0,1},{1,0},{2,3},{3,2},{4,5},{5,4},{6,7},{7,6},{8,9},{9,8},{10,11... | collective-permute-start | bytes 1179656 | tf_op jit(solution)/shard_map/ppermute | solution.py:436
  31.7 14.5 %collective-permute-start.28 = (bf16[384,512]{1,0:T(8,128)(2,1)S(1)}, bf16[384,512]{1,0:T(8,128)(2,1)S(1)}, u32[]{:S(2)}, u32[]{:S(2)}) collective-permute-start(bf16[384,512]{1,0:T(8,128)(2,1)S(1)} %collective-permute-done.24.refs_3_), channel_id=1, source_target_pairs={{0,1},{1,0},{2,3},{3,2},{4,5},{5,4},{6,7},{7,6},{8,9},{9,8},{10,11... | collective-permute-start | bytes 1179656 | tf_op jit(solution)/shard_map/ppermute | solution.py:436
  34.5 11.6 %all-to-all-start.2 = ((f32[32,1,1024]{2,1,0:T(1,128)}), f32[32,1,1024]{2,1,0:T(1,128)S(1)}, u32[]{:S(2)}, u32[]{:S(2)}) async-start(f32[32,1,1024]{2,1,0:T(1,128)} %get-tuple-element.143), calls=%async_computation.2 | async-start | bytes 262144 | tf_op jit(solution)/shard_map/all_to_all | solution.py:437
  37.6 8.6 %collective-permute-start.25 = (bf16[384,512]{1,0:T(8,128)(2,1)}, bf16[384,512]{1,0:T(8,128)(2,1)S(1)}, u32[]{:S(2)}, u32[]{:S(2)}) collective-permute-start(bf16[384,512]{1,0:T(8,128)(2,1)} %collective-permute-done.21.refs_0_), channel_id=1, source_target_pairs={{0,1},{1,0},{2,3},{3,2},{4,5},{5,4},{6,7},{7,6},{8,9},{9,8},{10,11... | collective-permute-start | bytes 1179656 | tf_op jit(solution)/shard_map/ppermute | solution.py:436
  39.9 6.3 %collective-permute-start.26 = (bf16[384,512]{1,0:T(8,128)(2,1)}, bf16[384,512]{1,0:T(8,128)(2,1)S(1)}, u32[]{:S(2)}, u32[]{:S(2)}) collective-permute-start(bf16[384,512]{1,0:T(8,128)(2,1)} %collective-permute-done.22.refs_1_), channel_id=1, source_target_pairs={{0,1},{1,0},{2,3},{3,2},{4,5},{5,4},{6,7},{7,6},{8,9},{9,8},{10,11... | collective-permute-start | bytes 1179656 | tf_op jit(solution)/shard_map/ppermute | solution.py:436
  41.4 8.4 %copy-start = (f32[256]{0:T(256)S(1)}, f32[256]{0:T(256)}, u32[]{:S(2)}) copy-start(f32[256]{0:T(256)} %param.8) | copy-start | bytes 3076
  49.8 20.0 %collective-permute-start.5 = (f32[128,512]{1,0:T(8,128)S(1)}, f32[128,512]{1,0:T(8,128)S(1)}, u32[]{:S(2)}, u32[]{:S(2)}) collective-permute-start(f32[128,512]{1,0:T(8,128)S(1)} %get-tuple-element.81.refs_0_), channel_id=1, source_target_pairs={{0,16},{1,17},{2,18},{3,19},{4,20},{5,21},{6,22},{7,23},{8,24},{9,... | collective-permute-start | bytes 786440 | tf_op jit(solution)/shard_map/cond/branch_0_fun/ppermute | solution.py:256
  53.1 22.2 %collective-permute-start = (f32[128,512]{1,0:T(8,128)S(1)}, f32[128,512]{1,0:T(8,128)S(1)}, u32[]{:S(2)}, u32[]{:S(2)}) collective-permute-start(f32[128,512]{1,0:T(8,128)S(1)} %get-tuple-element.78.refs_0_), channel_id=1, source_target_pairs={{0,16},{1,17},{2,18},{3,19},{4,20},{5,21},{6,22},{7,23},{8,24},{9,... | collective-permute-start | bytes 786440 | tf_op jit(solution)/shard_map/cond/branch_0_fun/ppermute | solution.py:256
  69.9 5.6 %collective-permute-start.6 = (bf16[1,128,512]{2,1,0:T(8,128)(2,1)S(1)}, bf16[1,128,512]{2,1,0:T(8,128)(2,1)S(1)}, u32[]{:S(2)}, u32[]{:S(2)}) collective-permute-start(bf16[1,128,512]{2,1,0:T(8,128)(2,1)S(1)} %bitcast.59), channel_id=1, source_target_pairs={{0,2},{1,5},{2,0},{3,7},{4,6},{5,1},{6,4},{7,3},{8,10},{9,13},{10,... | collective-permute-start | bytes 393224 | tf_op jit(solution)/shard_map/cond/branch_0_fun/ppermute | solution.py:256
  75.5 6.1 %collective-permute-start.1 = (bf16[1,128,512]{2,1,0:T(8,128)(2,1)S(1)}, bf16[1,128,512]{2,1,0:T(8,128)(2,1)S(1)}, u32[]{:S(2)}, u32[]{:S(2)}) collective-permute-start(bf16[1,128,512]{2,1,0:T(8,128)(2,1)S(1)} %bitcast.62), channel_id=1, source_target_pairs={{0,8},{1,5},{2,10},{3,7},{4,12},{5,1},{6,14},{7,3},{8,0},{9,13},{1... | collective-permute-start | bytes 393224 | tf_op jit(solution)/shard_map/cond/branch_0_fun/ppermute | solution.py:256
  75.6 8.2 %collective-permute-start.7 = (bf16[2,128,512]{2,1,0:T(8,128)(2,1)S(1)}, bf16[2,128,512]{2,1,0:T(8,128)(2,1)S(1)}, u32[]{:S(2)}, u32[]{:S(2)}) collective-permute-start(bf16[2,128,512]{2,1,0:T(8,128)(2,1)S(1)} %pad_maximum_fusion.1), channel_id=1, source_target_pairs={{0,4},{1,9},{2,6},{3,11},{4,0},{5,13},{6,2},{7,15},{8,12},{9,1},{1... | collective-permute-start | bytes 786440 | tf_op jit(solution)/shard_map/cond/branch_0_fun/ppermute | solution.py:256
  77.3 9.9 %collective-permute-start.8 = (bf16[2,128,512]{2,1,0:T(8,128)(2,1)S(1)}, bf16[2,128,512]{2,1,0:T(8,128)(2,1)S(1)}, u32[]{:S(2)}, u32[]{:S(2)}) collective-permute-start(bf16[2,128,512]{2,1,0:T(8,128)(2,1)S(1)} %pad_maximum_fusion.1), channel_id=1, source_target_pairs={{0,8},{1,3},{2,10},{3,1},{4,12},{5,7},{6,14},{7,5},{8,0},{9,11},{1... | collective-permute-start | bytes 786440 | tf_op jit(solution)/shard_map/cond/branch_0_fun/ppermute | solution.py:256
  81.6 7.3 %collective-permute-start.2 = (bf16[2,128,512]{2,1,0:T(8,128)(2,1)S(1)}, bf16[2,128,512]{2,1,0:T(8,128)(2,1)S(1)}, u32[]{:S(2)}, u32[]{:S(2)}) collective-permute-start(bf16[2,128,512]{2,1,0:T(8,128)(2,1)S(1)} %pad_maximum_fusion), channel_id=1, source_target_pairs={{0,2},{1,9},{2,0},{3,11},{4,6},{5,13},{6,4},{7,15},{8,10},{9,1},{1... | collective-permute-start | bytes 786440 | tf_op jit(solution)/shard_map/cond/branch_0_fun/ppermute | solution.py:256
  83.1 6.4 %collective-permute-start.3 = (bf16[2,128,512]{2,1,0:T(8,128)(2,1)S(1)}, bf16[2,128,512]{2,1,0:T(8,128)(2,1)S(1)}, u32[]{:S(2)}, u32[]{:S(2)}) collective-permute-start(bf16[2,128,512]{2,1,0:T(8,128)(2,1)S(1)} %pad_maximum_fusion), channel_id=1, source_target_pairs={{0,4},{1,3},{2,6},{3,1},{4,0},{5,7},{6,2},{7,5},{8,12},{9,11},{10,... | collective-permute-start | bytes 786440 | tf_op jit(solution)/shard_map/cond/branch_0_fun/ppermute | solution.py:256
  87.2 12.6 %collective-permute-start.9 = (bf16[2,128,512]{2,1,0:T(8,128)(2,1)S(1)}, bf16[2,128,512]{2,1,0:T(8,128)(2,1)S(1)}, u32[]{:S(2)}, u32[]{:S(2)}) collective-permute-start(bf16[2,128,512]{2,1,0:T(8,128)(2,1)S(1)} %collective-permute-done.7.refs_2_), channel_id=1, source_target_pairs={{0,8},{1,3},{2,10},{3,1},{4,12},{5,7},{6,14},{7,5},{8,0},{9,11},{1... | collective-permute-start | bytes 786440 | tf_op jit(solution)/shard_map/cond/branch_0_fun/ppermute | solution.py:256
  89.4 11.8 %collective-permute-start.4 = (bf16[2,128,512]{2,1,0:T(8,128)(2,1)S(1)}, bf16[2,128,512]{2,1,0:T(8,128)(2,1)S(1)}, u32[]{:S(2)}, u32[]{:S(2)}) collective-permute-start(bf16[2,128,512]{2,1,0:T(8,128)(2,1)S(1)} %collective-permute-done.2.refs_5_), channel_id=1, source_target_pairs={{0,4},{1,3},{2,6},{3,1},{4,0},{5,7},{6,2},{7,5},{8,12},{9,11},{10,... | collective-permute-start | bytes 786440 | tf_op jit(solution)/shard_map/cond/branch_0_fun/ppermute | solution.py:256
